TPU v7x, 32 devices: a whole 2x2x4 slice. The times are simulated.
32 devices in a mesh: group: 2 (over y), dom: 8 (over z, x), feat: 2 (over core).
Axes of the slice: x: 2, y: 2, z: 4, core: 2. Of those that a mesh axis runs over, the one named last changes fastest.
Arguments:
- features: bfloat16 [16384, 128], P(('group', 'dom')), parts along dimension 0, may hold values from -6 to 6
- w_self: bfloat16 [128, 256], P(None, 'feat'), may hold values from -0.5 to 0.5
- w_neigh: bfloat16 [128, 256], P(None, 'feat'), may hold values from -0.5 to 0.5
- bias: float32 [256], P('feat'), may hold values from -3 to 3
- cotangent: bfloat16 [16384, 256], P(('group', 'dom'), 'feat'), parts along dimension 0, may hold values from -6 to 6
- adjacency: bfloat16 [896, 256, 256], P(('group', 'dom')), parts along dimension 0, may hold values from -0.1875 to 0.1875
- tile_dst: int32 [896], P(('group', 'dom')), parts along dimension 0, may hold values from 0 to 3
- tile_src: int32 [896], P(('group', 'dom')), parts along dimension 0, may hold values from 0 to 5
- tile_count: int32 [16], P(('group', 'dom')), parts along dimension 0, may hold values from 1 to 56, 149 in all
- send_rows: int32 [16, 8, 2], P(('group', 'dom')), parts along dimension 0, may hold values from 0 to 1023
- send_count: int32 [16, 8], P(('group', 'dom')), parts along dimension 0, may hold values from 0 to 2, as said below
- hub_owner: int32 [32, 1], P('group'), parts along dimension 0, may hold values from 0 to 7; in each aligned block of 16 rows (0 to 15, 16 to 31, ...) at most 4 rows name the same one
- hub_row: int32 [32], P('group'), parts along dimension 0, may hold values from 0 to 1023
Outputs:
- output: bfloat16 [16384, 256], P(('group', 'dom'), 'feat'), parts along dimension 0
- grad_features: bfloat16 [16384, 128], P(('group', 'dom')), parts along dimension 0
- grad_w_self: float32 [256, 256], P('group', 'feat'), parts along dimension 0
- grad_w_neigh: float32 [256, 256], P('group', 'feat'), parts along dimension 0
- grad_bias: float32 [512], P(('group', 'feat')), parts along dimension 0
There are 2 independent parts, one for each index of `group`. A program takes and returns all parts, laid end to end along the dimension named above; an argument that names none is the same for every part. Nothing has to cross between parts.
Inputs may be any that keep to these rules, and one draw needn't show every extreme that they name: `send_count`: entry [q, p] is how many rows partition q sends to partition p; zero where q equals p; some partition receives 2 rows from every other partition. Only the first send_count[q, p] slots of send_rows[q, p] are sent. `hub_owner`: no partition owns more than 4 hubs, and some partition owns exactly 4. `tile_src`: source blocks 0 to 3 are the partition's own rows, then 1 block of received rows, then 1 block of hub rows. Tiles at position tile_count or later are not part of the graph; some partition uses all 56.
All inputs are finite; a program needn't handle non-finite values. No bound on the sum of `tile_count` on one device may be relied on, other than what follows from the above.
Results may differ from a plain program's by a relative error of at most 0.0058.
Values may be sent and summed in bfloat16 or wider, within the bound.
No kernel may reach another device: no remote copies, remote signals or barrier semaphores. Data moves between devices by JAX's collectives and lax.ppermute only.
A program may use at most 64 MiB of HBM per device.

v0:
```python
import jax
import jax.numpy as jnp
from jax import lax
from jax.sharding import PartitionSpec as P

HUB_MOST = 4


def activate(values):
    return jax.nn.gelu(values, approximate=True)


def activation_grad(preact, upstream):
    return jax.vjp(activate, preact)[1](upstream)[0]


def owner_slots(hub_owners):
    positions = jnp.arange(hub_owners.shape[0])
    same_owner = hub_owners[:, None] == hub_owners[None, :]
    earlier = positions[None, :] < positions[:, None]
    return jnp.sum(same_owner & earlier, axis=1)


def pad_rows(values, padded_rows):
    extra = padded_rows - values.shape[0]
    return jnp.concatenate([values, jnp.zeros((extra, values.shape[1]), values.dtype)], axis=0)


def local(
    features,
    w_self,
    w_neigh,
    bias,
    cotangent,
    adjacency,
    tile_dst,
    tile_src,
    tile_count,
    send_rows,
    send_count,
    hub_owner,
    hub_row,
):
    highest = lax.Precision.HIGHEST
    node_rows = features.shape[0]
    tile_rows = adjacency.shape[1]
    tile_limit = adjacency.shape[0]
    hidden_cols = w_neigh.shape[1]
    partitions = lax.axis_size("dom")
    own_index = lax.axis_index("dom")
    slot_count = send_rows.shape[2]
    hub_total = hub_row.shape[0]
    halo_rows = partitions * slot_count
    halo_padded = -(-halo_rows // tile_rows) * tile_rows
    hub_padded = -(-hub_total // tile_rows) * tile_rows
    dst_blocks = node_rows // tile_rows
    src_blocks = dst_blocks + (halo_padded + hub_padded) // tile_rows
    projected = jnp.dot(features, w_neigh, preferred_element_type=jnp.float32).astype(jnp.bfloat16)
    own_term = jnp.dot(features, w_self, preferred_element_type=jnp.float32)
    sent_mask = jnp.arange(slot_count)[None, :] < send_count[0][:, None]
    outgoing = jnp.where(
        sent_mask[:, :, None], projected[send_rows[0]], jnp.zeros((), jnp.bfloat16)
    )
    hub_owners = hub_owner[:, 0]
    owned = hub_owners == own_index
    hub_values = projected[hub_row]
    hub_slot = owner_slots(hub_owners)
    slot_match = owned[None, :] & (hub_slot[None, :] == jnp.arange(HUB_MOST)[:, None])
    packed = jnp.dot(
        slot_match.astype(jnp.bfloat16), hub_values, preferred_element_type=jnp.float32
    ).astype(jnp.bfloat16)
    bundle = jnp.concatenate(
        [outgoing, jnp.broadcast_to(packed[None], (partitions, HUB_MOST, hidden_cols))], axis=1
    )
    arrived = lax.all_to_all(bundle, "dom", split_axis=0, concat_axis=0, tiled=True)
    incoming = arrived[:, :slot_count]
    hub_table = arrived[:, slot_count:].reshape(partitions * HUB_MOST, hidden_cols)
    hub_block = hub_table[hub_owners * HUB_MOST + hub_slot]
    halo_block = pad_rows(incoming.reshape(halo_rows, hidden_cols), halo_padded)
    hub_block = pad_rows(hub_block, hub_padded)
    source = jnp.concatenate([projected, halo_block, hub_block], axis=0)
    blocks = source.reshape(src_blocks, tile_rows, hidden_cols)
    in_graph = jnp.arange(tile_limit) < tile_count[0]
    dst_select = (
        (tile_dst[None, :] == jnp.arange(dst_blocks)[:, None]) & in_graph[None, :]
    ).astype(jnp.float32)
    src_select = (
        (tile_src[None, :] == jnp.arange(src_blocks)[:, None]) & in_graph[None, :]
    ).astype(jnp.float32)
    chosen = blocks[tile_src]
    products = jnp.einsum("trs,tsi->tri", adjacency, chosen, preferred_element_type=jnp.float32)
    aggregate = jnp.einsum("dt,tri->dri", dst_select, products, precision=highest).reshape(
        node_rows, hidden_cols
    )
    preact = own_term + aggregate + bias[None, :]
    output = activate(preact).astype(jnp.bfloat16)
    grad_pre = activation_grad(preact, cotangent.astype(jnp.float32))
    grad_pre_low = grad_pre.astype(jnp.bfloat16)
    picked = grad_pre_low.reshape(dst_blocks, tile_rows, hidden_cols)[tile_dst]
    transposed = jnp.einsum("trs,tri->tsi", adjacency, picked, preferred_element_type=jnp.float32)
    grad_source = jnp.einsum("bt,tsi->bsi", src_select, transposed, precision=highest).reshape(
        -1, hidden_cols
    )
    grad_local = grad_source[:node_rows]
    grad_halo = grad_source[node_rows : node_rows + halo_rows].reshape(
        partitions, slot_count, hidden_cols
    )
    grad_hub = grad_source[node_rows + halo_padded : node_rows + halo_padded + hub_total]
    slot_rows = jnp.sum(jnp.where(slot_match, hub_row[None, :], 0), axis=1)
    filled = jnp.any(slot_match, axis=1)
    placed = (
        jnp.zeros((partitions * HUB_MOST, hidden_cols), jnp.float32)
        .at[hub_owners * HUB_MOST + hub_slot]
        .set(grad_hub)
    )
    bundle_back = jnp.concatenate(
        [grad_halo, placed.reshape(partitions, HUB_MOST, hidden_cols)], axis=1
    )
    arrived_back = lax.all_to_all(bundle_back, "dom", split_axis=0, concat_axis=0, tiled=True)
    returned = jnp.where(sent_mask[:, :, None], arrived_back[:, :slot_count], 0.0)
    owned_grads = jnp.sum(arrived_back[:, slot_count:], axis=0)
    grad_proj = grad_local.at[send_rows[0].reshape(-1)].add(returned.reshape(-1, hidden_cols))
    grad_proj = grad_proj.at[slot_rows].add(jnp.where(filled[:, None], owned_grads, 0.0))
    grad_proj_low = grad_proj.astype(jnp.bfloat16)
    contract_rows = (((0,), (0,)), ((), ()))
    contract_cols = (((1,), (1,)), ((), ()))
    term_self = lax.dot_general(
        features, grad_pre_low, contract_rows, preferred_element_type=jnp.float32
    )
    term_neigh = lax.dot_general(
        features, grad_proj_low, contract_rows, preferred_element_type=jnp.float32
    )
    term_bias = jnp.sum(grad_pre, axis=0)
    grad_w_self, grad_w_neigh, grad_bias = lax.psum((term_self, term_neigh, term_bias), "dom")
    partial_input = lax.dot_general(
        grad_pre_low, w_self, contract_cols, preferred_element_type=jnp.float32
    ) + lax.dot_general(grad_proj_low, w_neigh, contract_cols, preferred_element_type=jnp.float32)
    grad_features = lax.psum(partial_input, "feat").astype(jnp.bfloat16)
    return (output, grad_features, grad_w_self, grad_w_neigh, grad_bias)


def solution(mesh):
    return jax.shard_map(
        local,
        mesh=mesh,
        in_specs=(
            P(("group", "dom"), None),
            P(None, "feat"),
            P(None, "feat"),
            P("feat"),
            P(("group", "dom"), "feat"),
            P(("group", "dom"), None, None),
            P(("group", "dom")),
            P(("group", "dom")),
            P(("group", "dom")),
            P(("group", "dom"), None, None),
            P(("group", "dom"), None),
            P("group", None),
            P("group"),
        ),
        out_specs=(
            P(("group", "dom"), "feat"),
            P(("group", "dom"), None),
            P("group", "feat"),
            P("group", "feat"),
            P(("group", "feat")),
        ),
        check_vma=False,
    )
```

profile of v0, /device:TPU:0, one launch (start us, length us, event | category | flops | bytes accessed | tf_op | source)
XLA Modules:
  0.0 189.5 jit_solution(16134204613566021482)
XLA Ops:
  7.2 0.0 copy-start
  7.2 0.7 compare_select_fusion
  7.9 0.1 copy.39
  8.0 0.1 reshape.160
  8.1 0.7 compare_select_fusion.6
  8.7 0.9 convert_reduce_fusion
  9.6 0.7 broadcast_compare_fusion
  10.3 0.0 copy-done
  10.3 1.0 constant_dynamic-update-slice_fusion.2
  11.3 0.6 gather_fusion.1
  11.9 0.6 gather_fusion
  12.5 0.7 iota_compare_fusion.2
  13.2 0.1 broadcast_select_fusion
  13.3 0.1 convolution_convert_fusion.1
  13.4 0.6 pad_maximum_fusion.1
  14.0 7.3 %all-to-all-start = ((bf16[8,6,128]{2,1,0:T(8,128)(2,1)}), bf16[8,6,128]{2,1,0:T(8,128)(2,1)S(1)}, u32[]{:S(2)}, u32[]{:S(2)}) async-start(bf16[8,6,128]{2,1,0:T(8,128)(2,1)} %pad_maximum_fusion.1), calls=%async_computation | async-start | bytes 32768 | tf_op jit(solution)/shard_map/all_to_all | solution.py:75
  21.3 0.7 fusion.33
  21.9 0.8 copy.46
  22.7 0.8 select_reduce_fusion
  23.5 0.1 fusion.36
  23.6 0.7 compare_select_fusion.3
  24.2 0.7 compare_select_fusion.4
  25.6 0.1 reshape_squeeze.3
  25.7 2.2 %all-to-all-done = bf16[8,6,128]{2,1,0:T(8,128)(2,1)S(1)} async-done(((bf16[8,6,128]{2,1,0:T(8,128)(2,1)}), bf16[8,6,128]{2,1,0:T(8,128)(2,1)S(1)}, u32[]{:S(2)}, u32[]{:S(2)}) %all-to-all-start) | async-done | bytes 12320 | tf_op jit(solution)/shard_map/all_to_all | solution.py:75
  27.9 0.6 gather_fusion.2
  28.5 3.0 %gather_fusion.3 = bf16[56,256,128]{2,1,0:T(8,128)(2,1)} fusion(bf16[6,256,128]{2,1,0:T(8,128)(2,1)S(1)} %bitcast.64, s32[1024]{0:T(1024)S(1)} %get-tuple-element.33), kind=kCustom, calls=%fused_computation.3 | custom fusion | bytes 7340256 | tf_op jit(solution)/shard_map/gather | solution.py:90
  31.5 9.7 %convolution_bitcast_fusion.1 = f32[56,256,128]{1,2,0:T(8,128)} fusion(bf16[56,256,128]{2,1,0:T(8,128)(2,1)} %gather_fusion.3, bf16[56,256,256]{2,1,0:T(8,128)(2,1)} %param.18), kind=kOutput, calls=%fused_computation.9 | convolution fusion | flops 939524096 | bytes 18350080 | tf_op jit(solution)/shard_map/trs,tsi->tri/dot_general | solution.py:91
  41.2 0.0 copy-start.3
  41.2 7.9 %copy.41 = f32[56,256,128]{2,0,1:T(8,128)} copy(f32[56,256,128]{1,2,0:T(8,128)} %convolution_bitcast_fusion.1) | data formatting | bytes 14680064 | tf_op jit(solution)/shard_map/trs,tsi->tri/dot_general | solution.py:91
  49.1 0.0 copy-done.3
  49.1 0.0 copy-start.2
  49.1 0.0 copy-start.5
  49.1 0.0 copy-start.6
  49.1 5.6 %fusion.25 = f32[4,256,128]{2,0,1:T(4,128)S(1)} fusion(f32[56,256,128]{2,0,1:T(8,128)} %copy.41, s32[56]{0:T(128)S(1)} %copy-done.3, pred[56]{0:T(512)(128)(4,1)S(1)} %iota_compare_fusion.5), kind=kOutput, calls=%fused_computation.74 | convolution fusion | flops 88080832 | bytes 7864600 | tf_op jit(solution)/shard_map/dt,tri->dri/dot_general | solution.py:92
  54.8 0.0 copy-done.2
  54.8 0.0 copy-done.5
  54.8 0.0 copy-done.6
  54.8 1.3 fusion.38
  56.2 0.2 fusion.40
  56.4 3.0 %gather_fusion.4 = bf16[56,256,128]{2,1,0:T(8,128)(2,1)} fusion(bf16[4,256,128]{2,1,0:T(8,128)(2,1)S(1)} %bitcast.63, s32[1024]{0:T(1024)S(1)} %get-tuple-element.32), kind=kCustom, calls=%fused_computation.4 | custom fusion | bytes 7340256 | tf_op jit(solution)/shard_map/gather | solution.py:99
  59.4 8.5 %convolution_bitcast_fusion = f32[56,256,128]{1,2,0:T(8,128)} fusion(bf16[56,256,128]{2,1,0:T(8,128)(2,1)} %gather_fusion.4, bf16[56,256,256]{2,1,0:T(8,128)(2,1)} %param.18), kind=kOutput, calls=%fused_computation.8 | convolution fusion | flops 939524096 | bytes 18350080 | tf_op jit(solution)/shard_map/trs,tri->tsi/dot_general | solution.py:100
  67.9 7.9 %copy.44 = f32[56,256,128]{2,0,1:T(8,128)} copy(f32[56,256,128]{1,2,0:T(8,128)} %convolution_bitcast_fusion) | data formatting | bytes 14680064 | tf_op jit(solution)/shard_map/trs,tri->tsi/dot_general | solution.py:100
  75.8 0.0 copy-done.4
  75.8 4.7 %fusion.18 = f32[6,256,128]{2,0,1:T(8,128)S(1)} fusion(f32[56,256,128]{2,0,1:T(8,128)} %copy.44, s32[56]{0:T(128)S(1)} %copy-done.4, pred[56]{0:T(512)(128)(4,1)S(1)} %iota_compare_fusion.5), kind=kOutput, calls=%fused_computation.58 | convolution fusion | flops 132121248 | bytes 8126744 | tf_op jit(solution)/shard_map/bt,tsi->bsi/dot_general | solution.py:101
  80.5 0.2 copy.47
  80.7 0.6 scatter_custom_fusion
  81.3 0.6 pad_maximum_fusion
  81.9 3.8 %all-to-all-start.1 = ((f32[8,6,128]{2,1,0:T(8,128)}), f32[8,6,128]{2,1,0:T(8,128)S(1)}, u32[]{:S(2)}, u32[]{:S(2)}) async-start(f32[8,6,128]{2,1,0:T(8,128)} %pad_maximum_fusion), calls=%async_computation.1 | async-start | bytes 65536 | tf_op jit(solution)/shard_map/all_to_all | solution.py:119
  85.8 0.0 all-reduce.4.cloned.1.call-start
  85.8 0.9 convolution_bitcast_fusion.3
  86.7 0.1 slice.44
  86.9 22.3 %psum.31 = f32[128]{0:T(128)} all-reduce(f32[128]{0:T(128)S(1)} %get-tuple-element.27), channel_id=1, replica_groups=mesh['group'=2,'dom'=8,'feat'=2] {'dom'}, use_global_device_ids=true, to_apply=%region_11.12 | all-reduce | flops 128 | bytes 1024 | tf_op jit(solution)/shard_map/psum | solution.py:134
  109.2 0.0 all-to-all-done.1
  109.2 0.1 slice_select_fusion
  109.3 0.9 scatter_fusion
  110.1 0.9 scatter_custom_fusion.2
  111.0 0.9 convolution_bitcast_fusion.2
  111.9 0.0 copy-done.1
  112.0 0.2 convolution_add_fusion
  112.2 0.0 all-reduce.4.cloned.1.call-update
  112.2 5.3 %all-reduce.5 = bf16[1024,128]{1,0:T(8,128)(2,1)} all-reduce(f32[1024,128]{1,0:T(8,128)S(1)} %convolution_add_fusion), channel_id=1, replica_groups=mesh['group'=2,'dom'=8,'feat'=2] {'feat'}, use_global_device_ids=true, to_apply=%region_7.8 | all-reduce | flops 131072 | bytes 786432 | tf_op jit(solution)/shard_map/psum | solution.py:138
  117.5 62.0 %all-reduce.4.cloned.1.call-done = (f32[128,128]{0,1:T(8,128)}, f32[128,128]{0,1:T(8,128)}) async-done(((f32[128,128]{0,1:T(8,128)}, f32[128,128]{0,1:T(8,128)}), (f32[128,128]{0,1:T(8,128)}, f32[128,128]{0,1:T(8,128)})) %all-reduce.4.cloned.1.call-update) | async-done | bytes 131088 | tf_op jit(solution)/shard_map/psum | solution.py:134
  179.6 1.6 copy.48
  181.1 1.6 copy.49
  (19 shorter events, 0.2 us)
Async XLA Ops:
  7.2 3.1 %copy-start = (bf16[1024,128]{1,0:T(8,128)(2,1)S(1)}, bf16[1024,128]{1,0:T(8,128)(2,1)}, u32[]{:S(2)}) copy-start(bf16[1024,128]{1,0:T(8,128)(2,1)} %param.13) | copy-start | bytes 786436
  14.0 13.8 %all-to-all-start = ((bf16[8,6,128]{2,1,0:T(8,128)(2,1)}), bf16[8,6,128]{2,1,0:T(8,128)(2,1)S(1)}, u32[]{:S(2)}, u32[]{:S(2)}) async-start(bf16[8,6,128]{2,1,0:T(8,128)(2,1)} %pad_maximum_fusion.1), calls=%async_computation | async-start | bytes 32768 | tf_op jit(solution)/shard_map/all_to_all | solution.py:75
  41.2 7.9 %copy-start.3 = (s32[56]{0:T(128)S(1)}, s32[56]{0:T(128)}, u32[]{:S(2)}) copy-start(s32[56]{0:T(128)} %param.19) | copy-start | bytes 676
  49.1 5.7 %copy-start.2 = (bf16[128,128]{1,0:T(8,128)(2,1)S(1)}, bf16[128,128]{1,0:T(8,128)(2,1)}, u32[]{:S(2)}) copy-start(bf16[128,128]{1,0:T(8,128)(2,1)} %param.14) | copy-start | bytes 98308
  49.1 5.7 %copy-start.5 = (bf16[1024,128]{1,0:T(8,128)(2,1)S(1)}, bf16[1024,128]{1,0:T(8,128)(2,1)}, u32[]{:S(2)}) copy-start(bf16[1024,128]{1,0:T(8,128)(2,1)} %param.17) | copy-start | bytes 786436
  49.1 5.7 %copy-start.6 = (f32[128]{0:T(128)S(1)}, f32[128]{0:T(128)}, u32[]{:S(2)}) copy-start(f32[128]{0:T(128)} %param.16) | copy-start | bytes 1540
  67.9 7.9 %copy-start.4 = (s32[56]{0:T(128)S(1)}, s32[56]{0:T(128)}, u32[]{:S(2)}) copy-start(s32[56]{0:T(128)} %param.20) | copy-start | bytes 676
  75.8 36.1 %copy-start.1 = (bf16[128,128]{1,0:T(8,128)(2,1)S(1)}, bf16[128,128]{1,0:T(8,128)(2,1)}, u32[]{:S(2)}) copy-start(bf16[128,128]{1,0:T(8,128)(2,1)} %param.15) | copy-start | bytes 98308
  81.9 27.2 %all-to-all-start.1 = ((f32[8,6,128]{2,1,0:T(8,128)}), f32[8,6,128]{2,1,0:T(8,128)S(1)}, u32[]{:S(2)}, u32[]{:S(2)}) async-start(f32[8,6,128]{2,1,0:T(8,128)} %pad_maximum_fusion), calls=%async_computation.1 | async-start | bytes 65536 | tf_op jit(solution)/shard_map/all_to_all | solution.py:119
  85.8 93.8 %all-reduce.4.cloned.1.call-start = ((), (), s32[]{:S(2)}) async-start(), calls=%async_computation.2 | async-start | bytes 262144 | tf_op jit(solution)/shard_map/psum | solution.py:134
Sparse Core Ops, SparseCore 0:
  112.3 67.1 all-reduce.3
where the time goes:
time: 190 us
  waiting for transfers between devices  64.2 us (34%)
  matrix products  33.2 us (17%)
  local copies, waits for them, and re-layouts  28.7 us (15%)
  blocking collectives  27.6 us (15%)
  between operations  14.9 us (8%)
  starting transfers between devices  11.1 us (6%)
  other arithmetic  9.77 us (5%)
    psum x1, waiting for transfers between devices, local(): lax.psum((term_self, term_neigh, term_bias), 'dom')  62 us
    psum x1, blocking collectives, local(): lax.psum((term_self, term_neigh, term_bias), 'dom')  22.3 us
    dot_general x1, matrix products, local(): jnp.einsum('trs,tsi->tri', adjacency, chosen, preferred_element_type=jnp....  9.71 us
    dot_general x1, matrix products, local(): jnp.einsum('trs,tri->tsi', adjacency, picked, preferred_element_type=jnp....  8.54 us
    dot_general x1, local copies, waits for them, and re-layouts, local(): jnp.einsum('trs,tsi->tri', adjacency, chosen, preferred_element_type=jnp....  7.91 us
    dot_general x1, local copies, waits for them, and re-layouts, local(): jnp.einsum('trs,tri->tsi', adjacency, picked, preferred_element_type=jnp....  7.91 us
    all_to_all x1, starting transfers between devices, local(): lax.all_to_all(bundle, 'dom', split_axis=0, concat_axis=0, tiled=True)  7.26 us
    dot_general x1, matrix products, local(): jnp.einsum('dt,tri->dri', dst_select, products, precision=highest)  5.64 us
  transfers between devices with their start and end apart: 3, of which 2 were waited for; matrix products, arithmetic and copies ran while one was open for 3% of the time, Pallas kernels for 0%

commit v1 on v0

v1 whole, which is shorter than its diff:
```python
import functools

import jax
import jax.numpy as jnp
from jax import lax
from jax.experimental import pallas as pl
from jax.experimental.pallas import tpu as pltpu
from jax.sharding import PartitionSpec as P

HUB_MOST = 4
PEER_ROWS = 8
GROUP_TILES = 8
F32 = jnp.float32
BF16 = jnp.bfloat16
NT = (((1,), (1,)), ((), ()))


def dot(a, b):
    return jnp.dot(a, b, preferred_element_type=F32)


def dot_nt(a, b):
    return lax.dot_general(a, b, NT, preferred_element_type=F32)


def repeat(count, body, init):
    return lax.fori_loop(0, count, body, init, unroll=True)


def hub_slots(owner_ref, counter_ref, partitions, body):
    def clear(q, carry):
        counter_ref[q] = 0
        return carry

    def visit(hub, carry):
        owner = owner_ref[hub]
        slot = counter_ref[owner]
        counter_ref[owner] = slot + 1
        body(hub, owner, slot)
        return carry

    repeat(partitions, clear, 0)
    repeat(owner_ref.shape[0], visit, 0)


def fetch(pairs, sems):
    copies = [pltpu.make_async_copy(src, dst, sems.at[k]) for k, (src, dst) in enumerate(pairs)]
    for copy in copies:
        copy.start()
    return copies


def gather_kernel(
    rows_hbm, count_hbm, owner_hbm, hub_row_hbm, features_hbm,
    bundle_ref,
    rows_ref, count_ref, owner_ref, hub_row_ref, features_ref, wide_ref, hubs_ref, sems,
):
    own = lax.axis_index("dom")
    partitions = bundle_ref.shape[0]
    slots = rows_ref.shape[0]
    copies = fetch(
        [
            (features_hbm, features_ref), (rows_hbm, rows_ref), (count_hbm, count_ref),
            (owner_hbm, owner_ref), (hub_row_hbm, hub_row_ref),
        ],
        sems,
    )
    hubs_ref[...] = jnp.zeros_like(hubs_ref)
    for copy in copies:
        copy.wait()
    wide_ref[...] = features_ref[...].astype(F32)

    def hub(index, slot):
        mine = owner_ref[index] == own

        @pl.when(mine)
        def _():
            hubs_ref[pl.ds(slots + slot, 1), :] = wide_ref[pl.ds(hub_row_ref[index], 1), :]

        return slot + mine.astype(jnp.int32)

    repeat(owner_ref.shape[0], hub, jnp.int32(0))

    def peer(q, carry):
        bundle_ref[q] = hubs_ref[...]
        for slot in range(slots):
            row = wide_ref[pl.ds(rows_ref[slot, q], 1), :]
            bundle_ref[q, slot : slot + 1, :] = jnp.where(slot < count_ref[q], row, 0.0)
        return carry

    repeat(partitions, peer, 0)


def put(list_ref, position, tile, dst, src):
    list_ref[0, position] = tile
    list_ref[1, position] = dst
    list_ref[2, position] = src


def split_tiles(near_ref, far_ref, dst_ref, src_ref, count, split):
    def visit(tile, used):
        src, dst = src_ref[tile], dst_ref[tile]
        near, far = used
        put(near_ref, near, tile, dst, src)
        put(far_ref, far, tile, dst, src)
        is_near = (src < split).astype(jnp.int32)
        return near + is_near, far + 1 - is_near

    return lax.fori_loop(0, count, visit, (jnp.int32(0), jnp.int32(0)))


def pad_list(list_ref, used, dst, src):
    first = list_ref[0, 0]
    for k in range(GROUP_TILES):
        put(list_ref, used + k, first, dst, src)


class Tiles:
    def __init__(self, list_ref, total, source, held, sems):
        self.list_ref, self.total, self.source, self.held, self.sems = list_ref, total, source, held, sems

    def copy(self, position):
        tile = self.list_ref[0, position]
        return pltpu.make_async_copy(self.source.at[tile], self.held.at[tile], self.sems.at[tile])

    def start(self):
        def one(position, carry):
            self.copy(position).start()
            return carry

        lax.fori_loop(0, self.total, one, 0)

    def each(self, body, wait):
        def group(step, carry):
            if wait:
                for k in range(GROUP_TILES):
                    position = step * GROUP_TILES + k

                    @pl.when(position < self.total)
                    def _(position=position):
                        self.copy(position).wait()

            for k in range(GROUP_TILES):
                position = step * GROUP_TILES + k
                tile = self.held[self.list_ref[0, position]]
                body(tile, self.list_ref[1, position], self.list_ref[2, position])
            return carry

        lax.fori_loop(0, (self.total + GROUP_TILES - 1) // GROUP_TILES, group, 0)


def own_kernel(
    dst_hbm, src_hbm, count_hbm, features_hbm, w_self_hbm, w_neigh_hbm, bias_hbm, adjacency_hbm,
    total_ref,
    dst_ref, src_ref, count_ref, features_ref, w_self_ref, w_neigh_ref, bias_ref,
    adjacency_ref, blocks_ref, list_ref, far_list_ref, sems, tile_sems,
):
    tile_rows = adjacency_ref.shape[1]
    dst_blocks = total_ref.shape[0] - 1
    copies = fetch(
        [
            (src_hbm, src_ref), (dst_hbm, dst_ref), (count_hbm, count_ref), (w_neigh_hbm, w_neigh_ref),
            (features_hbm, features_ref), (w_self_hbm, w_self_ref), (bias_hbm, bias_ref),
        ],
        sems,
    )
    for copy in copies[:3]:
        copy.wait()
    used, _ = split_tiles(list_ref, far_list_ref, dst_ref, src_ref, count_ref[0], dst_blocks)
    pad_list(list_ref, used, dst_blocks, dst_blocks)
    tiles = Tiles(list_ref, used, adjacency_hbm, adjacency_ref, tile_sems)
    tiles.start()
    for copy in copies[3:]:
        copy.wait()
    features = features_ref[...]
    projected = dot(features, w_neigh_ref[...]).astype(BF16)
    for block in range(dst_blocks):
        blocks_ref[block] = projected[block * tile_rows : (block + 1) * tile_rows]
    blocks_ref[dst_blocks] = jnp.zeros(blocks_ref.shape[1:], BF16)
    base = dot(features, w_self_ref[...]) + bias_ref[...]
    for block in range(dst_blocks):
        total_ref[block] = base[block * tile_rows : (block + 1) * tile_rows]
    total_ref[dst_blocks] = jnp.zeros(total_ref.shape[1:], F32)

    def forward(tile, dst, src):
        total_ref[dst] += dot(tile, blocks_ref[src])

    tiles.each(forward, wait=True)


def rest_kernel(
    dst_ref, src_ref, count_ref, owner_ref,
    arrived_ref, total_hbm, features_ref, w_self_ref, w_neigh_ref, cotangent_ref, adjacency_hbm,
    output_ref, partial_ref, pack_ref,
    total_ref, rows_ref, low_rows_ref, blocks_ref, grad_ref, grad_t_ref, source_t_ref, back_ref,
    adjacency_ref, far_list_ref, own_list_ref, counter_ref, tile_sems, total_sem,
    *, partitions, slots,
):
    tile_rows = adjacency_ref.shape[1]
    dst_blocks = total_hbm.shape[0] - 1
    halo_blocks = -(-partitions * slots // tile_rows)
    hub_blocks = -(-owner_ref.shape[0] // tile_rows)
    extra_blocks = halo_blocks + hub_blocks
    hub_base = halo_blocks * tile_rows
    source_blocks = dst_blocks + extra_blocks
    fetch_total = pltpu.make_async_copy(total_hbm, total_ref, total_sem)
    fetch_total.start()
    near_used, far_used = split_tiles(own_list_ref, far_list_ref, dst_ref, src_ref, count_ref[0], dst_blocks)
    far = Tiles(far_list_ref, far_used, adjacency_hbm, adjacency_ref, tile_sems)
    far.start()
    own = Tiles(own_list_ref, near_used, adjacency_hbm, adjacency_ref, tile_sems)
    own.start()
    pad_list(far_list_ref, far_used, dst_blocks, source_blocks)
    pad_list(own_list_ref, near_used, dst_blocks, source_blocks)

    rows_ref[...] = jnp.zeros_like(rows_ref)

    def halo_in(q, carry):
        rows_ref[pl.ds(q * slots, slots), :] = arrived_ref[q, 0:slots, :]
        return carry

    repeat(partitions, halo_in, 0)

    def hub_in(hub, owner, slot):
        rows_ref[pl.ds(hub_base + hub, 1), :] = arrived_ref[owner, pl.ds(slots + slot, 1), :]

    hub_slots(owner_ref, counter_ref, partitions, hub_in)
    low_rows_ref[...] = rows_ref[...].astype(BF16)
    for block in range(extra_blocks):
        rows = low_rows_ref[block * tile_rows : (block + 1) * tile_rows]
        blocks_ref[block] = dot(rows, w_neigh_ref[...]).astype(BF16)
    blocks_ref[extra_blocks] = jnp.zeros(blocks_ref.shape[1:], BF16)
    fetch_total.wait()

    def forward(tile, dst, src):
        total_ref[dst] += dot(tile, blocks_ref[src - dst_blocks])

    far.each(forward, wait=True)

    root = 0.7978845608028654
    bias_sum = jnp.zeros((1, output_ref.shape[1]), F32)
    w_self_t = jnp.zeros((output_ref.shape[1], features_ref.shape[1]), F32)
    for block in range(dst_blocks):
        span = slice(block * tile_rows, (block + 1) * tile_rows)
        v = total_ref[block]
        square = v * v
        gate = jnp.tanh(root * (v + 0.044715 * (v * square)))
        half = 0.5 * (1.0 + gate)
        output_ref[span, :] = (v * half).astype(BF16)
        slope = half + (0.5 * root) * v * (1.0 - gate * gate) * (1.0 + (3 * 0.044715) * square)
        grad = cotangent_ref[span, :].astype(F32) * slope
        bias_sum += jnp.sum(grad, axis=0, keepdims=True)
        low = grad.astype(BF16)
        grad_ref[block] = low
        low_t = jnp.transpose(grad).astype(BF16)
        grad_t_ref[block] = low_t
        w_self_t += dot(low_t, features_ref[span, :])
    grad_t_ref[dst_blocks] = jnp.zeros(grad_t_ref.shape[1:], BF16)

    source_t_ref[...] = jnp.zeros_like(source_t_ref)

    def backward(tile, dst, src):
        source_t_ref[src] += dot(grad_t_ref[dst], tile)

    far.each(backward, wait=False)
    own.each(backward, wait=True)

    w_neigh_t = jnp.zeros_like(w_self_t)
    for block in range(dst_blocks):
        span = slice(block * tile_rows, (block + 1) * tile_rows)
        source_t = source_t_ref[block]
        w_neigh_t += dot(source_t.astype(BF16), features_ref[span, :])
        partial_ref[span, :] = dot_nt(grad_ref[block], w_self_ref[...]) + dot_nt(
            jnp.transpose(source_t).astype(BF16), w_neigh_ref[...]
        )
    for block in range(extra_blocks):
        span = slice(block * tile_rows, (block + 1) * tile_rows)
        source_t = source_t_ref[dst_blocks + block]
        w_neigh_t += dot(source_t.astype(BF16), low_rows_ref[span, :])
        back_ref[span, :] = dot_nt(jnp.transpose(source_t).astype(BF16), w_neigh_ref[...])

    w_self = jnp.transpose(w_self_t)
    w_neigh = jnp.transpose(w_neigh_t)
    share = w_self.shape[0] // partitions
    for q in range(partitions):
        pack_ref[q, PEER_ROWS : PEER_ROWS + share, :] = w_self[q * share : (q + 1) * share]
        pack_ref[q, PEER_ROWS + share : PEER_ROWS + 2 * share, :] = w_neigh[q * share : (q + 1) * share]

    def halo_out(q, carry):
        pack_ref[q, 0:PEER_ROWS, :] = jnp.zeros((PEER_ROWS, pack_ref.shape[2]), F32)
        pack_ref[q, 0:slots, :] = back_ref[pl.ds(q * slots, slots), :]
        pack_ref[q, PEER_ROWS - 1 : PEER_ROWS, :] = bias_sum
        return carry

    repeat(partitions, halo_out, 0)

    def hub_out(hub, owner, slot):
        pack_ref[owner, pl.ds(slots + slot, 1), :] = back_ref[pl.ds(hub_base + hub, 1), :]

    hub_slots(owner_ref, counter_ref, partitions, hub_out)


def merge_kernel(
    rows_ref, count_ref, owner_ref, hub_row_ref, arrived_ref, partial_ref,
    share_ref, bias_ref, low_ref, total_ref, hubs_ref,
):
    own = lax.axis_index("dom")
    partitions = arrived_ref.shape[0]
    slots = rows_ref.shape[0]
    summed = jnp.sum(arrived_ref[...], axis=0)
    bias_ref[...] = summed[PEER_ROWS - 1 : PEER_ROWS]
    hubs_ref[...] = summed[0:PEER_ROWS]
    shares = summed[PEER_ROWS:]
    for q in range(partitions):
        share_ref[q] = shares
    total_ref[...] = partial_ref[...]

    def peer(q, carry):
        for slot in range(slots):
            row = pl.ds(rows_ref[slot, q], 1)
            total_ref[row, :] += jnp.where(slot < count_ref[q], arrived_ref[q, slot : slot + 1, :], 0.0)
        return carry

    repeat(partitions, peer, 0)

    def hub(index, slot):
        mine = owner_ref[index] == own

        @pl.when(mine)
        def _():
            total_ref[pl.ds(hub_row_ref[index], 1), :] += hubs_ref[pl.ds(slots + slot, 1), :]

        return slot + mine.astype(jnp.int32)

    repeat(owner_ref.shape[0], hub, jnp.int32(0))
    low_ref[...] = total_ref[...].astype(BF16)


SMEM = pl.BlockSpec(memory_space=pltpu.SMEM)
VMEM = pl.BlockSpec(memory_space=pltpu.VMEM)
HBM = pl.BlockSpec(memory_space=pltpu.HBM)


def call(kernel, name, ins, outs, scratch, args, grant, flops=0, size=0):
    return pl.pallas_call(
        kernel,
        out_shape=outs,
        in_specs=ins,
        out_specs=jax.tree.map(lambda _: VMEM, outs),
        scratch_shapes=scratch,
        compiler_params=pltpu.CompilerParams(vmem_limit_bytes=grant * 1024 * 1024),
        cost_estimate=pl.CostEstimate(flops=flops, bytes_accessed=size, transcendentals=0),
        name=name,
    )(*args)


def local(
    features, w_self, w_neigh, bias, cotangent, adjacency, tile_dst, tile_src, tile_count,
    send_rows, send_count, hub_owner, hub_row,
):
    nodes, inputs = features.shape
    limit, tile_rows, _ = adjacency.shape
    hidden = w_neigh.shape[1]
    partitions = lax.axis_size("dom")
    slots = send_rows.shape[2]
    hubs = hub_row.shape[0]
    dst_blocks = nodes // tile_rows
    extra_blocks = -(-partitions * slots // tile_rows) - (-hubs // tile_rows)
    share = inputs // partitions
    rows = jnp.transpose(send_rows[0])
    counts = send_count.reshape(partitions)
    owner = hub_owner.reshape(hubs)
    struct = jax.ShapeDtypeStruct
    lists = pltpu.SMEM((3, limit + GROUP_TILES), jnp.int32)

    bundle = call(
        gather_kernel, "gather", [HBM] * 5,
        struct((partitions, PEER_ROWS, inputs), F32),
        [
            pltpu.SMEM((slots, partitions), jnp.int32),
            pltpu.SMEM((partitions,), jnp.int32),
            pltpu.SMEM((hubs,), jnp.int32),
            pltpu.SMEM((hubs,), jnp.int32),
            pltpu.VMEM((nodes, inputs), BF16),
            pltpu.VMEM((nodes, inputs), F32),
            pltpu.VMEM((PEER_ROWS, inputs), F32),
            pltpu.SemaphoreType.DMA((5,)),
        ],
        (rows, counts, owner, hub_row, features), 60,
    )
    arrived = lax.all_to_all(bundle, "dom", split_axis=0, concat_axis=0, tiled=True)
    total = call(
        own_kernel, "own_tiles", [HBM] * 8,
        struct((dst_blocks + 1, tile_rows, hidden), F32),
        [
            pltpu.SMEM((limit,), jnp.int32),
            pltpu.SMEM((limit,), jnp.int32),
            pltpu.SMEM((1,), jnp.int32),
            pltpu.VMEM((nodes, inputs), BF16),
            pltpu.VMEM((inputs, hidden), BF16),
            pltpu.VMEM((inputs, hidden), BF16),
            pltpu.VMEM((1, hidden), F32),
            pltpu.VMEM(adjacency.shape, BF16),
            pltpu.VMEM((dst_blocks + 1, tile_rows, hidden), BF16),
            lists,
            lists,
            pltpu.SemaphoreType.DMA((7,)),
            pltpu.SemaphoreType.DMA((limit,)),
        ],
        (tile_dst, tile_src, tile_count, features, w_self, w_neigh, bias.reshape(1, hidden), adjacency), 54,
        flops=2 * limit * tile_rows * tile_rows * hidden, size=adjacency.size * 2,
    )
    output, partial, pack = call(
        functools.partial(rest_kernel, partitions=partitions, slots=slots), "rest",
        [SMEM] * 4 + [VMEM, HBM] + [VMEM] * 4 + [HBM],
        (
            struct((nodes, hidden), BF16),
            struct((nodes, inputs), F32),
            struct((partitions, PEER_ROWS + 2 * share, inputs), F32),
        ),
        [
            pltpu.VMEM((dst_blocks + 1, tile_rows, hidden), F32),
            pltpu.VMEM((extra_blocks * tile_rows, inputs), F32),
            pltpu.VMEM((extra_blocks * tile_rows, inputs), BF16),
            pltpu.VMEM((extra_blocks + 1, tile_rows, hidden), BF16),
            pltpu.VMEM((dst_blocks, tile_rows, hidden), BF16),
            pltpu.VMEM((dst_blocks + 1, hidden, tile_rows), BF16),
            pltpu.VMEM((dst_blocks + extra_blocks + 1, hidden, tile_rows), F32),
            pltpu.VMEM((extra_blocks * tile_rows, inputs), F32),
            pltpu.VMEM(adjacency.shape, BF16),
            lists,
            lists,
            pltpu.SMEM((partitions,), jnp.int32),
            pltpu.SemaphoreType.DMA((limit,)),
            pltpu.SemaphoreType.DMA,
        ],
        (tile_dst, tile_src, tile_count, owner, arrived, total, features, w_self, w_neigh, cotangent, adjacency), 50,
    )
    returned = lax.all_to_all(pack, "dom", split_axis=0, concat_axis=0, tiled=True)
    shares, grad_bias, low = call(
        merge_kernel, "merge", [SMEM] * 4 + [VMEM] * 2,
        (
            struct((partitions, 2 * share, inputs), F32),
            struct((1, inputs), F32),
            struct((nodes, inputs), BF16),
        ),
        [pltpu.VMEM((nodes, inputs), F32), pltpu.VMEM((PEER_ROWS, inputs), F32)],
        (rows, counts, owner, hub_row, returned, partial), 32,
    )
    gathered = lax.all_to_all(shares, "dom", split_axis=0, concat_axis=0, tiled=True)
    other = lax.ppermute(low, "feat", [(0, 1), (1, 0)])
    grad_features = (low.astype(F32) + other.astype(F32)).astype(BF16)
    grad_w_self = gathered[:, :share].reshape(inputs, hidden)
    grad_w_neigh = gathered[:, share:].reshape(inputs, hidden)
    return (output, grad_features, grad_w_self, grad_w_neigh, grad_bias.reshape(hidden))


def solution(mesh):
    return jax.shard_map(
        local,
        mesh=mesh,
        in_specs=(
            P(("group", "dom"), None),
            P(None, "feat"),
            P(None, "feat"),
            P("feat"),
            P(("group", "dom"), "feat"),
            P(("group", "dom"), None, None),
            P(("group", "dom")),
            P(("group", "dom")),
            P(("group", "dom")),
            P(("group", "dom"), None, None),
            P(("group", "dom"), None),
            P("group", None),
            P("group"),
        ),
        out_specs=(
            P(("group", "dom"), "feat"),
            P(("group", "dom"), None),
            P("group", "feat"),
            P("group", "feat"),
            P(("group", "feat")),
        ),
        check_vma=False,
    )
```

time: 190 us -> 53.7 us (0.28)
  waiting for transfers between devices: 64.2 us -> 8.52 us
  matrix products: 33.2 us -> 0 us
  local copies, waits for them, and re-layouts: 28.7 us -> 1.8 us
  Pallas kernels: 0 us -> 14.1 us
  between operations: 14.9 us -> 1.45 us
  blocking collectives: 27.6 us -> 16.4 us
  other arithmetic: 9.77 us -> 0.77 us
    psum x1 -> x0, waiting for transfers between devices: 62 us -> none  [local(): lax.psum((term_self, term_neigh, term_bias), 'dom')]
    dot_general x11 -> x0, matrix products: 33.2 us -> none  [the longest x1 9.71 us: local(): jnp.einsum('trs,tsi->tri', adjacency, chosen, preferred_element_type=jnp....]
    psum x2 -> x0, blocking collectives: 27.6 us -> none  [the longest x1 22.3 us: local(): lax.psum((term_self, term_neigh, term_bias), 'dom')]
    all_to_all x0 -> x1, blocking collectives: none -> 16.4 us  [local(): lax.all_to_all(pack, 'dom', split_axis=0, concat_axis=0, tiled=True)]
    dot_general x4 -> x0, local copies, waits for them, and re-layouts: 16 us -> none  [the longest x1 7.91 us: local(): jnp.einsum('trs,tsi->tri', adjacency, chosen, preferred_element_type=jnp....]
    pallas_call x0 -> x4, Pallas kernels: none -> 14.1 us  [call(): pl.pallas_call(kernel, out_shape=outs, in_specs=ins, out_specs=jax.tree.m...]
    gather x5 -> x0, local copies, waits for them, and re-layouts: 7.67 us -> none  [the longest x1 2.98 us: local(): picked = grad_pre_low.reshape(dst_blocks, tile_rows, hidden_cols)[tile_dst]]
    all_to_all x1, waiting for transfers between devices: 0.01 us -> 7.2 us  [local(): lax.all_to_all(shares, 'dom', split_axis=0, concat_axis=0, tiled=True)]
  transfers between devices with their start and end apart: 3 -> 3, of which waited for: 2 -> 2; matrix products, arithmetic and copies ran while one was open for 3% -> 1% of each run, Pallas kernels for 0% -> 9%
where the time goes in v1:
time: 53.7 us
  blocking collectives  16.4 us (31%)
  Pallas kernels  14.1 us (26%)
  starting transfers between devices  10.7 us (20%)
  waiting for transfers between devices  8.52 us (16%)
  local copies, waits for them, and re-layouts  1.8 us (3%)
  between operations  1.45 us (3%)
  other arithmetic  0.77 us (1%)
    all_to_all x1, blocking collectives, local(): lax.all_to_all(pack, 'dom', split_axis=0, concat_axis=0, tiled=True)  16.4 us
    pallas_call x4, Pallas kernels, call(): pl.pallas_call(kernel, out_shape=outs, in_specs=ins, out_specs=jax.tree.m...  14.1 us
    all_to_all x1, starting transfers between devices, local(): lax.all_to_all(bundle, 'dom', split_axis=0, concat_axis=0, tiled=True)  7.27 us
    all_to_all x1, waiting for transfers between devices, local(): lax.all_to_all(shares, 'dom', split_axis=0, concat_axis=0, tiled=True)  7.2 us
    all_to_all x1, starting transfers between devices, local(): lax.all_to_all(shares, 'dom', split_axis=0, concat_axis=0, tiled=True)  3.37 us
    all_to_all x1, waiting for transfers between devices, local(): lax.all_to_all(bundle, 'dom', split_axis=0, concat_axis=0, tiled=True)  1.32 us
    unnamed x22, local copies, waits for them, and re-layouts  1.14 us
  transfers between devices with their start and end apart: 3, of which 2 were waited for; matrix products, arithmetic and copies ran while one was open for 1% of the time, Pallas kernels for 9%

profile of v1, /device:TPU:0, one launch (start us, length us, event | category | flops | bytes accessed | tf_op | source)
XLA Modules:
  0.0 53.7 jit_solution(17657051359435423554)
XLA Ops:
  0.6 0.0 copy-start.1
  0.6 0.0 copy-start.5
  0.7 0.0 copy-start.8
  0.7 0.0 copy-start.7
  0.7 0.0 copy-start.4
  0.7 0.0 copy-start.3
  0.7 0.0 copy-start.2
  0.7 1.9 %gather.1 = f32[8,8,128]{2,1,0:T(8,128)} custom-call(s32[2,8]{1,0:T(2,128)} %bitcast.12, s32[8]{0:T(128)} %bitcast.14, s32[16]{0:T(128)} %bitcast.9, s32[16]{0:T(128)} %hub_row_ref.1, bf16[1024,128]{1,0:T(8,128)(2,1)} %features_ref.1), custom_call_target="tpu_custom_call" | custom-call | tf_op jit(solution)/shard_map/gather/pallas_call | solution.py:345
  2.7 7.3 %all-to-all-start = ((f32[8,8,128]{2,1,0:T(8,128)}), f32[8,8,128]{2,1,0:T(8,128)S(1)}, u32[]{:S(2)}, u32[]{:S(2)}) async-start(f32[8,8,128]{2,1,0:T(8,128)} %gather.1), calls=%async_computation | async-start | bytes 65536 | tf_op jit(solution)/shard_map/all_to_all | solution.py:391
  10.6 0.0 copy-start.6
  10.6 0.0 copy-start.9
  10.6 0.0 copy-start.10
  10.6 4.7 %own_tiles.1.total_hbm = f32[5,256,128]{2,1,0:T(8,128)} custom-call(s32[56]{0:T(128)} %dst_ref.1, s32[56]{0:T(128)} %src_ref.1, s32[1]{0:T(128)S(6)} %copy.18.count_hbm.count_ref, bf16[1024,128]{1,0:T(8,128)(2,1)} %features_ref.1, bf16[128,128]{1,0:T(8,128)(2,1)} %w_self_ref.1, bf16[128,128]{1,0:T(8,128)(2,1)} %w_neigh_ref.1, f32[1,128]{1,0:T(1,128)} %bitcast.18, ...), custom_call_target="tpu_custom_call" | custom-call | flops 939524096 | bytes 7340032 | tf_op jit(solution)/shard_map/own_tiles/pallas_call | solution.py:345
  15.3 1.3 %all-to-all-done.arrived_ref = f32[8,8,128]{2,1,0:T(8,128)S(1)} async-done(((f32[8,8,128]{2,1,0:T(8,128)}), f32[8,8,128]{2,1,0:T(8,128)S(1)}, u32[]{:S(2)}, u32[]{:S(2)}) %all-to-all-start) | async-done | bytes 32800 | tf_op jit(solution)/shard_map/all_to_all | solution.py:391
  16.6 0.0 copy-done.1
  16.6 0.0 copy-done.5
  16.6 0.0 copy-done.8
  16.6 0.0 copy-done.7
  16.6 0.0 copy-done.4
  16.6 0.0 copy-done.3
  16.7 0.0 copy-done.2
  16.7 0.0 copy-start
  16.7 1.1 %copy-done = f32[5,256,128]{2,1,0:T(8,128)S(1)} copy-done((f32[5,256,128]{2,1,0:T(8,128)S(1)}, f32[5,256,128]{2,1,0:T(8,128)}, u32[]{:S(2)}) %copy-start) | copy-done | bytes 655384
  17.8 6.0 %rest.1 = (bf16[1024,128]{1,0:T(8,128)(2,1)}, f32[1024,128]{1,0:T(8,128)S(1)}, f32[8,40,128]{2,1,0:T(8,128)S(1)}) custom-call(s32[56]{0:T(128)S(1)} %copy-done.7, s32[56]{0:T(128)S(1)} %copy-done.8, s32[1]{0:T(128)S(6)} %copy.18.count_hbm.count_ref, s32[16]{0:T(128)S(1)} %bitcast.10, f32[8,8,128]{2,1,0:T(8,128)S(1)} %all-to-all-done.arrived_ref, ...), custom_call_target="tpu_custom_call" | custom-call | tf_op jit(solution)/shard_map/rest/pallas_call | solution.py:345
  23.8 16.4 %all_to_all.15.arrived_ref = f32[8,40,128]{2,1,0:T(8,128)S(1)} all-to-all(f32[8,40,128]{2,1,0:T(8,128)S(1)} %get-tuple-element.12), channel_id=1, replica_groups=mesh['group'=2,'dom'=8,'feat'=2] {'dom'}, dimensions={0} | all-to-all | bytes 327680 | tf_op jit(solution)/shard_map/all_to_all | solution.py:439
  40.1 0.0 copy-done.6
  40.1 0.0 copy-done.9
  40.1 0.0 copy-done.10
  40.1 1.5 %merge.1 = (f32[8,32,128]{2,1,0:T(8,128)}, f32[1,128]{1,0:T(1,128)}, bf16[1024,128]{1,0:T(8,128)(2,1)S(1)}) custom-call(s32[2,8]{1,0:T(2,128)S(1)} %bitcast.13, s32[8]{0:T(128)S(1)} %bitcast.15, s32[16]{0:T(128)S(1)} %bitcast.11, s32[16]{0:T(128)S(1)} %copy-done.10, f32[8,40,128]{2,1,0:T(8,128)S(1)} %all_to_all.15.arrived_ref, ...), custom_call_target="tpu_custom_call" | custom-call | tf_op jit(solution)/shard_map/merge/pallas_call | solution.py:345
  41.6 3.4 %all-to-all-start.2 = ((f32[8,32,128]{2,1,0:T(8,128)}), f32[8,32,128]{2,1,0:T(8,128)S(1)}, u32[]{:S(2)}, u32[]{:S(2)}) async-start(f32[8,32,128]{2,1,0:T(8,128)} %get-tuple-element.15), calls=%async_computation.2 | async-start | bytes 262144 | tf_op jit(solution)/shard_map/all_to_all | solution.py:450
  45.0 0.1 collective-permute-start
  45.1 7.2 %all-to-all-done.2 = f32[8,32,128]{2,1,0:T(8,128)S(1)} async-done(((f32[8,32,128]{2,1,0:T(8,128)}), f32[8,32,128]{2,1,0:T(8,128)S(1)}, u32[]{:S(2)}, u32[]{:S(2)}) %all-to-all-start.2) | async-done | bytes 131104 | tf_op jit(solution)/shard_map/all_to_all | solution.py:450
  52.3 0.7 %fusion = (f32[8,16,128]{2,1,0:T(8,128)}, f32[8,16,128]{2,1,0:T(8,128)}) fusion(f32[8,32,128]{2,1,0:T(8,128)S(1)} %all-to-all-done.2), kind=kLoop, calls=%fused_computation.1 | loop fusion | bytes 262144 | tf_op jit(solution)/shard_map/slice | solution.py:454
  52.9 0.0 collective-permute-done
  52.9 0.8 %add_convert_fusion = bf16[1024,128]{1,0:T(8,128)(2,1)} fusion(bf16[1024,128]{1,0:T(8,128)(2,1)S(1)} %collective-permute-done, bf16[1024,128]{1,0:T(8,128)(2,1)S(1)} %get-tuple-element.14), kind=kLoop, calls=%fused_computation | loop fusion | flops 524288 | bytes 786432 | tf_op jit(solution)/shard_map/convert_element_type | solution.py:452
Async XLA Ops:
  0.6 16.0 %copy-start.1 = (bf16[1024,128]{1,0:T(8,128)(2,1)S(1)}, bf16[1024,128]{1,0:T(8,128)(2,1)}, u32[]{:S(2)}) copy-start(bf16[1024,128]{1,0:T(8,128)(2,1)} %features_ref.1) | copy-start | bytes 786436
  0.6 16.0 %copy-start.5 = (s32[16,1]{0,1:T(1,128)S(1)}, s32[16,1]{0,1:T(1,128)}, u32[]{:S(2)}) copy-start(s32[16,1]{0,1:T(1,128)} %param.24) | copy-start | bytes 196
  0.7 16.0 %copy-start.8 = (s32[56]{0:T(128)S(1)}, s32[56]{0:T(128)}, u32[]{:S(2)}) copy-start(s32[56]{0:T(128)} %src_ref.1) | copy-start | bytes 676
  0.7 16.0 %copy-start.7 = (s32[56]{0:T(128)S(1)}, s32[56]{0:T(128)}, u32[]{:S(2)}) copy-start(s32[56]{0:T(128)} %dst_ref.1) | copy-start | bytes 676
  0.7 16.0 %copy-start.4 = (bf16[128,128]{1,0:T(8,128)(2,1)S(1)}, bf16[128,128]{1,0:T(8,128)(2,1)}, u32[]{:S(2)}) copy-start(bf16[128,128]{1,0:T(8,128)(2,1)} %w_neigh_ref.1) | copy-start | bytes 98308
  0.7 16.0 %copy-start.3 = (bf16[128,128]{1,0:T(8,128)(2,1)S(1)}, bf16[128,128]{1,0:T(8,128)(2,1)}, u32[]{:S(2)}) copy-start(bf16[128,128]{1,0:T(8,128)(2,1)} %w_self_ref.1) | copy-start | bytes 98308
  0.7 16.0 %copy-start.2 = (bf16[1024,128]{1,0:T(8,128)(2,1)S(1)}, bf16[1024,128]{1,0:T(8,128)(2,1)}, u32[]{:S(2)}) copy-start(bf16[1024,128]{1,0:T(8,128)(2,1)} %cotangent_ref.1) | copy-start | bytes 786436
  2.7 14.0 %all-to-all-start = ((f32[8,8,128]{2,1,0:T(8,128)}), f32[8,8,128]{2,1,0:T(8,128)S(1)}, u32[]{:S(2)}, u32[]{:S(2)}) async-start(f32[8,8,128]{2,1,0:T(8,128)} %gather.1), calls=%async_computation | async-start | bytes 65536 | tf_op jit(solution)/shard_map/all_to_all | solution.py:391
  10.6 29.6 %copy-start.6 = (s32[1,8,2]{1,2,0:T(2,128)S(1)}, s32[1,8,2]{1,2,0:T(2,128)}, u32[]{:S(2)}) copy-start(s32[1,8,2]{1,2,0:T(2,128)} %param.22) | copy-start | bytes 196
  10.6 29.5 %copy-start.9 = (s32[1,8]{1,0:T(1,128)S(1)}, s32[1,8]{1,0:T(1,128)}, u32[]{:S(2)}) copy-start(s32[1,8]{1,0:T(1,128)} %param.23) | copy-start | bytes 100
  10.6 29.5 %copy-start.10 = (s32[16]{0:T(128)S(1)}, s32[16]{0:T(128)}, u32[]{:S(2)}) copy-start(s32[16]{0:T(128)} %hub_row_ref.1) | copy-start | bytes 196
  16.7 1.1 %copy-start = (f32[5,256,128]{2,1,0:T(8,128)S(1)}, f32[5,256,128]{2,1,0:T(8,128)}, u32[]{:S(2)}) copy-start(f32[5,256,128]{2,1,0:T(8,128)} %own_tiles.1.total_hbm) | copy-start | bytes 1966084
  41.6 10.7 %all-to-all-start.2 = ((f32[8,32,128]{2,1,0:T(8,128)}), f32[8,32,128]{2,1,0:T(8,128)S(1)}, u32[]{:S(2)}, u32[]{:S(2)}) async-start(f32[8,32,128]{2,1,0:T(8,128)} %get-tuple-element.15), calls=%async_computation.2 | async-start | bytes 262144 | tf_op jit(solution)/shard_map/all_to_all | solution.py:450
  45.0 7.9 %collective-permute-start = (bf16[1024,128]{1,0:T(8,128)(2,1)S(1)}, bf16[1024,128]{1,0:T(8,128)(2,1)S(1)}, u32[]{:S(2)}, u32[]{:S(2)}) collective-permute-start(bf16[1024,128]{1,0:T(8,128)(2,1)S(1)} %get-tuple-element.14), channel_id=1, source_target_pairs={{0,1},{1,0},{2,3},{3,2},{4,5},{5,4},{6,7},{7,6},{8,9},{9,8},{10,11... | collective-permute-start | bytes 786440 | tf_op jit(solution)/shard_map/ppermute | solution.py:451

commit v2 on v1

--- a/solution.py
+++ b/solution.py
@@ -191,11 +191,12 @@
 def rest_kernel(
     dst_ref, src_ref, count_ref, owner_ref,
     arrived_ref, total_hbm, features_ref, w_self_ref, w_neigh_ref, cotangent_ref, adjacency_hbm,
-    output_ref, partial_ref, pack_ref,
-    total_ref, rows_ref, low_rows_ref, blocks_ref, grad_ref, grad_t_ref, source_t_ref, back_ref,
+    output_ref, partial_ref, message_ref, keep_ref,
+    halo_ref, hubs_ref, total_ref, rows_ref, low_rows_ref, blocks_ref, grad_ref, grad_t_ref, source_t_ref, back_ref,
     adjacency_ref, far_list_ref, own_list_ref, counter_ref, tile_sems, total_sem,
     *, partitions, slots,
 ):
+    me = lax.axis_index("dom")
     tile_rows = adjacency_ref.shape[1]
     dst_blocks = total_hbm.shape[0] - 1
     halo_blocks = -(-partitions * slots // tile_rows)
@@ -279,56 +280,113 @@
         w_neigh_t += dot(source_t.astype(BF16), low_rows_ref[span, :])
         back_ref[span, :] = dot_nt(jnp.transpose(source_t).astype(BF16), w_neigh_ref[...])
 
-    w_self = jnp.transpose(w_self_t)
-    w_neigh = jnp.transpose(w_neigh_t)
-    share = w_self.shape[0] // partitions
-    for q in range(partitions):
-        pack_ref[q, PEER_ROWS : PEER_ROWS + share, :] = w_self[q * share : (q + 1) * share]
-        pack_ref[q, PEER_ROWS + share : PEER_ROWS + 2 * share, :] = w_neigh[q * share : (q + 1) * share]
-
     def halo_out(q, carry):
-        pack_ref[q, 0:PEER_ROWS, :] = jnp.zeros((PEER_ROWS, pack_ref.shape[2]), F32)
-        pack_ref[q, 0:slots, :] = back_ref[pl.ds(q * slots, slots), :]
-        pack_ref[q, PEER_ROWS - 1 : PEER_ROWS, :] = bias_sum
+        halo_ref[pl.ds((q ^ me) * slots, slots), :] = back_ref[pl.ds(q * slots, slots), :]
         return carry
 
     repeat(partitions, halo_out, 0)
+    hubs_ref[...] = jnp.zeros_like(hubs_ref)
 
     def hub_out(hub, owner, slot):
-        pack_ref[owner, pl.ds(slots + slot, 1), :] = back_ref[pl.ds(hub_base + hub, 1), :]
+        hubs_ref[pl.ds((owner ^ me) * HUB_MOST + slot, 1), :] = back_ref[pl.ds(hub_base + hub, 1), :]
 
     hub_slots(owner_ref, counter_ref, partitions, hub_out)
-
-
-def merge_kernel(
-    rows_ref, count_ref, owner_ref, hub_row_ref, arrived_ref, partial_ref,
-    share_ref, bias_ref, low_ref, total_ref, hubs_ref,
+    plan = Exchange(partitions, slots, 0)
+    message_ref[0 : plan.weights, :] = jnp.concatenate([w_self_t, w_neigh_t], axis=0).astype(BF16)
+    plan.write(message_ref, keep_ref, halo_ref[...], hubs_ref[...], bias_sum)
+
+
+class Exchange:
+    weights = 256
+
+    def __init__(self, partitions, slots, step):
+        self.groups = 1 << step
+        self.half = partitions >> (step + 1)
+        self.slots = slots
+        self.halo = self.groups * self.half * slots
+        self.hub = self.half * HUB_MOST
+        self.keep = self.halo + self.hub
+        self.rows = self.weights + -(-(self.keep + 2) // 16) * 16
+
+    def halves(self, rows, width):
+        lower, upper = [], []
+        span = self.half * width
+        for group in range(rows.shape[0] // (2 * span)):
+            base = 2 * group * span
+            lower.append(rows[base : base + span])
+            upper.append(rows[base + span : base + 2 * span])
+        return lower, upper
+
+    def write(self, message_ref, keep_ref, halo, hubs, bias):
+        halo_keep, halo_send = self.halves(halo, self.slots)
+        hub_keep, hub_send = self.halves(hubs, HUB_MOST)
+        high = bias.astype(BF16).astype(F32)
+        spare = self.rows - self.weights - self.keep - 2
+        parts = halo_send + hub_send + [high, bias - high]
+        if spare:
+            parts.append(jnp.zeros((spare, bias.shape[1]), F32))
+        message_ref[self.weights : self.rows, :] = jnp.concatenate(parts, axis=0).astype(BF16)
+        keep_ref[...] = jnp.concatenate(halo_keep + hub_keep, axis=0)
+
+    def tail(self, ref):
+        return ref[self.weights : self.rows, :].astype(F32)
+
+    def bias(self, own, other):
+        k = self.keep
+        return (own[k : k + 1] + own[k + 1 : k + 2]) + (other[k : k + 1] + other[k + 1 : k + 2])
+
+    def merged(self, keep, other):
+        halo = jnp.concatenate([keep[: self.halo], other[: self.halo]], axis=0)
+        return halo, keep[self.halo :] + other[self.halo : self.keep]
+
+    def weight_sum(self, sent_ref, got_ref):
+        rows = slice(0, self.weights)
+        return sent_ref[rows, :].astype(F32) + got_ref[rows, :].astype(F32)
+
+
+def step_kernel(sent_ref, got_ref, keep_ref, message_ref, next_keep_ref, *, now, then):
+    message_ref[0 : now.weights, :] = now.weight_sum(sent_ref, got_ref).astype(BF16)
+    other = now.tail(got_ref)
+    halo, hubs = now.merged(keep_ref[...], other)
+    then.write(message_ref, next_keep_ref, halo, hubs, now.bias(now.tail(sent_ref), other))
+
+
+def returned_kernel(got_ref, keep_ref, rows_ref, *, now):
+    halo, hubs = now.merged(keep_ref[...], now.tail(got_ref))
+    rows_ref[...] = jnp.concatenate([halo, hubs], axis=0)
+
+
+def weights_kernel(sent_ref, got_ref, w_self_ref, w_neigh_ref, bias_ref, *, now):
+    total = now.weight_sum(sent_ref, got_ref)
+    split = now.weights // 2
+    w_self_ref[...] = jnp.transpose(total[:split])
+    w_neigh_ref[...] = jnp.transpose(total[split:])
+    bias_ref[...] = now.bias(now.tail(sent_ref), now.tail(got_ref))
+
+
+def features_kernel(
+    rows_ref, count_ref, owner_ref, hub_row_ref, partial_ref, other_partial_ref, own_rows_ref, other_rows_ref,
+    low_ref, total_ref, returned_ref,
 ):
-    own = lax.axis_index("dom")
-    partitions = arrived_ref.shape[0]
-    slots = rows_ref.shape[0]
-    summed = jnp.sum(arrived_ref[...], axis=0)
-    bias_ref[...] = summed[PEER_ROWS - 1 : PEER_ROWS]
-    hubs_ref[...] = summed[0:PEER_ROWS]
-    shares = summed[PEER_ROWS:]
-    for q in range(partitions):
-        share_ref[q] = shares
-    total_ref[...] = partial_ref[...]
-
-    def peer(q, carry):
+    me = lax.axis_index("dom")
+    slots, partitions = rows_ref.shape
+    steps = partitions.bit_length() - 1
+    total_ref[...] = partial_ref[...] + other_partial_ref[...]
+    returned_ref[...] = own_rows_ref[...] + other_rows_ref[...]
+
+    for group in range(partitions):
+        origin = me ^ sum(((group >> k) & 1) << (steps - 1 - k) for k in range(steps))
         for slot in range(slots):
-            row = pl.ds(rows_ref[slot, q], 1)
-            total_ref[row, :] += jnp.where(slot < count_ref[q], arrived_ref[q, slot : slot + 1, :], 0.0)
-        return carry
-
-    repeat(partitions, peer, 0)
+            row = pl.ds(rows_ref[slot, origin], 1)
+            place = group * slots + slot
+            total_ref[row, :] += jnp.where(slot < count_ref[origin], returned_ref[place : place + 1, :], 0.0)
 
     def hub(index, slot):
-        mine = owner_ref[index] == own
+        mine = owner_ref[index] == me
 
         @pl.when(mine)
         def _():
-            total_ref[pl.ds(hub_row_ref[index], 1), :] += hubs_ref[pl.ds(slots + slot, 1), :]
+            total_ref[pl.ds(hub_row_ref[index], 1), :] += returned_ref[pl.ds(partitions * slots + slot, 1), :]
 
         return slot + mine.astype(jnp.int32)
 
@@ -366,7 +424,6 @@
     hubs = hub_row.shape[0]
     dst_blocks = nodes // tile_rows
     extra_blocks = -(-partitions * slots // tile_rows) - (-hubs // tile_rows)
-    share = inputs // partitions
     rows = jnp.transpose(send_rows[0])
     counts = send_count.reshape(partitions)
     owner = hub_owner.reshape(hubs)
@@ -410,15 +467,19 @@
         (tile_dst, tile_src, tile_count, features, w_self, w_neigh, bias.reshape(1, hidden), adjacency), 54,
         flops=2 * limit * tile_rows * tile_rows * hidden, size=adjacency.size * 2,
     )
-    output, partial, pack = call(
+    plans = [Exchange(partitions, slots, step) for step in range(partitions.bit_length() - 1)]
+    output, partial, message, keep = call(
         functools.partial(rest_kernel, partitions=partitions, slots=slots), "rest",
         [SMEM] * 4 + [VMEM, HBM] + [VMEM] * 4 + [HBM],
         (
             struct((nodes, hidden), BF16),
             struct((nodes, inputs), F32),
-            struct((partitions, PEER_ROWS + 2 * share, inputs), F32),
+            struct((plans[0].rows, inputs), BF16),
+            struct((plans[0].keep, inputs), F32),
         ),
         [
+            pltpu.VMEM((partitions * slots, inputs), F32),
+            pltpu.VMEM((partitions * HUB_MOST, inputs), F32),
             pltpu.VMEM((dst_blocks + 1, tile_rows, hidden), F32),
             pltpu.VMEM((extra_blocks * tile_rows, inputs), F32),
             pltpu.VMEM((extra_blocks * tile_rows, inputs), BF16),
@@ -436,22 +497,32 @@
         ],
         (tile_dst, tile_src, tile_count, owner, arrived, total, features, w_self, w_neigh, cotangent, adjacency), 50,
     )
-    returned = lax.all_to_all(pack, "dom", split_axis=0, concat_axis=0, tiled=True)
-    shares, grad_bias, low = call(
-        merge_kernel, "merge", [SMEM] * 4 + [VMEM] * 2,
-        (
-            struct((partitions, 2 * share, inputs), F32),
-            struct((1, inputs), F32),
-            struct((nodes, inputs), BF16),
-        ),
-        [pltpu.VMEM((nodes, inputs), F32), pltpu.VMEM((PEER_ROWS, inputs), F32)],
-        (rows, counts, owner, hub_row, returned, partial), 32,
-    )
-    gathered = lax.all_to_all(shares, "dom", split_axis=0, concat_axis=0, tiled=True)
-    other = lax.ppermute(low, "feat", [(0, 1), (1, 0)])
-    grad_features = (low.astype(F32) + other.astype(F32)).astype(BF16)
-    grad_w_self = gathered[:, :share].reshape(inputs, hidden)
-    grad_w_neigh = gathered[:, share:].reshape(inputs, hidden)
+    other_partial = lax.ppermute(partial, "feat", [(0, 1), (1, 0)])
+    for now in plans:
+        got = lax.ppermute(message, "dom", [(q, q ^ now.half) for q in range(partitions)])
+        if now is plans[-1]:
+            break
+        then = plans[plans.index(now) + 1]
+        message, keep = call(
+            functools.partial(step_kernel, now=now, then=then), "step", [VMEM] * 3,
+            (struct((then.rows, inputs), BF16), struct((then.keep, inputs), F32)),
+            [], (message, got, keep), 16,
+        )
+    own_rows = call(
+        functools.partial(returned_kernel, now=now), "returned", [VMEM] * 2,
+        struct((2 * now.halo + now.hub, inputs), F32), [], (got, keep), 16,
+    )
+    other_rows = lax.ppermute(own_rows, "feat", [(0, 1), (1, 0)])
+    grad_w_self, grad_w_neigh, grad_bias = call(
+        functools.partial(weights_kernel, now=now), "weights", [VMEM] * 2,
+        (struct((inputs, hidden), F32), struct((inputs, hidden), F32), struct((1, hidden), F32)),
+        [], (message, got), 16,
+    )
+    grad_features = call(
+        features_kernel, "features", [SMEM] * 4 + [VMEM] * 4, struct((nodes, inputs), BF16),
+        [pltpu.VMEM((nodes, inputs), F32), pltpu.VMEM((2 * now.halo + now.hub, inputs), F32)],
+        (rows, counts, owner, hub_row, partial, other_partial, own_rows, other_rows), 32,
+    )
     return (output, grad_features, grad_w_self, grad_w_neigh, grad_bias.reshape(hidden))
 
 

time: 53.7 us -> 45.5 us (0.85)
  blocking collectives: 16.4 us -> 0 us
  waiting for transfers between devices: 8.52 us -> 14.2 us
  starting transfers between devices: 10.7 us -> 15.4 us
  Pallas kernels: 14.1 us -> 13.2 us
  other arithmetic: 0.77 us -> 0 us
  local copies, waits for them, and re-layouts: 1.8 us -> 1.14 us
    all_to_all x1 -> x0, blocking collectives: 16.4 us -> none  [local(): lax.all_to_all(pack, 'dom', split_axis=0, concat_axis=0, tiled=True)]
    ppermute x1 -> x5, waiting for transfers between devices: 0.01 us -> 11.9 us  [the longest x3 11.5 us: local(): lax.ppermute(message, 'dom', [(q, q ^ now.half) for q in range(partitions)])]
    ppermute x1 -> x5, starting transfers between devices: 0.07 us -> 8.17 us  [the longest x3 8.1 us: local(): lax.ppermute(message, 'dom', [(q, q ^ now.half) for q in range(partitions)])]
    all_to_all x1 -> x0, waiting for transfers between devices: 7.2 us -> none  [local(): lax.all_to_all(shares, 'dom', split_axis=0, concat_axis=0, tiled=True)]
    all_to_all x1 -> x0, starting transfers between devices: 3.37 us -> none  [local(): lax.all_to_all(shares, 'dom', split_axis=0, concat_axis=0, tiled=True)]
    all_to_all x1, waiting for transfers between devices: 1.32 us -> 2.25 us  [local(): lax.all_to_all(bundle, 'dom', split_axis=0, concat_axis=0, tiled=True)]
    pallas_call x4 -> x8, Pallas kernels: 14.1 us -> 13.2 us  [call(): pl.pallas_call(kernel, out_shape=outs, in_specs=ins, out_specs=jax.tree.m...]
    convert_element_type x1 -> x0, other arithmetic: 0.77 us -> none  [local(): grad_features = (low.astype(F32) + other.astype(F32)).astype(BF16)]
  transfers between devices with their start and end apart: 3 -> 6, of which waited for: 2 -> 5; matrix products, arithmetic and copies ran while one was open for 1% -> 0% of each run, Pallas kernels for 9% -> 10%
where the time goes in v2:
time: 45.5 us; the launch traced here: 45.4 us
  starting transfers between devices  15.4 us (34%)
  waiting for transfers between devices  14.2 us (31%)
  Pallas kernels  13.2 us (29%)
  between operations  1.47 us (3%)
  local copies, waits for them, and re-layouts  1.14 us (3%)
    pallas_call x8, Pallas kernels, call(): pl.pallas_call(kernel, out_shape=outs, in_specs=ins, out_specs=jax.tree.m...  13.2 us
    ppermute x3, waiting for transfers between devices, local(): lax.ppermute(message, 'dom', [(q, q ^ now.half) for q in range(partitions)])  11.5 us
    ppermute x3, starting transfers between devices, local(): lax.ppermute(message, 'dom', [(q, q ^ now.half) for q in range(partitions)])  8.1 us
    all_to_all x1, starting transfers between devices, local(): lax.all_to_all(bundle, 'dom', split_axis=0, concat_axis=0, tiled=True)  7.27 us
    all_to_all x1, waiting for transfers between devices, local(): lax.all_to_all(bundle, 'dom', split_axis=0, concat_axis=0, tiled=True)  2.25 us
    unnamed x22, local copies, waits for them, and re-layouts  1.14 us
  transfers between devices with their start and end apart: 6, of which 5 were waited for; matrix products, arithmetic and copies ran while one was open for 0% of the time, Pallas kernels for 10%

profile of v2, /device:TPU:0, one launch (start us, length us, event | category | flops | bytes accessed | tf_op | source)
XLA Modules:
  0.0 45.4 jit_solution(8071847879668512462)
XLA Ops:
  0.6 0.0 copy-start.1
  0.6 0.0 copy-start.5
  0.7 0.0 copy-start.10
  0.7 0.0 copy-start.9
  0.7 0.0 copy-start.4
  0.7 0.0 copy-start.3
  0.7 0.0 copy-start.2
  0.7 1.9 %gather.1 = f32[8,8,128]{2,1,0:T(8,128)} custom-call(s32[2,8]{1,0:T(2,128)} %bitcast.10, s32[8]{0:T(128)} %bitcast.12, s32[16]{0:T(128)} %bitcast.7, s32[16]{0:T(128)} %hub_row_ref.1, bf16[1024,128]{1,0:T(8,128)(2,1)} %features_ref.1), custom_call_target="tpu_custom_call" | custom-call | tf_op jit(solution)/shard_map/gather/pallas_call | solution.py:403
  2.7 7.3 %all-to-all-start = ((f32[8,8,128]{2,1,0:T(8,128)}), f32[8,8,128]{2,1,0:T(8,128)S(1)}, u32[]{:S(2)}, u32[]{:S(2)}) async-start(f32[8,8,128]{2,1,0:T(8,128)} %gather.1), calls=%async_computation | async-start | bytes 65536 | tf_op jit(solution)/shard_map/all_to_all | solution.py:448
  10.6 0.0 copy-start.6
  10.6 0.0 copy-start.7
  10.6 0.0 copy-start.8
  10.6 3.7 %own_tiles.1.total_hbm = f32[5,256,128]{2,1,0:T(8,128)} custom-call(s32[56]{0:T(128)} %dst_ref.1, s32[56]{0:T(128)} %src_ref.1, s32[1]{0:T(128)S(6)} %copy.18.count_hbm.count_ref, bf16[1024,128]{1,0:T(8,128)(2,1)} %features_ref.1, bf16[128,128]{1,0:T(8,128)(2,1)} %w_self_ref.1, bf16[128,128]{1,0:T(8,128)(2,1)} %w_neigh_ref.1, f32[1,128]{1,0:T(1,128)} %bitcast.14, ...), custom_call_target="tpu_custom_call" | custom-call | flops 939524096 | bytes 7340032 | tf_op jit(solution)/shard_map/own_tiles/pallas_call | solution.py:403
  14.4 2.3 %all-to-all-done.arrived_ref = f32[8,8,128]{2,1,0:T(8,128)S(1)} async-done(((f32[8,8,128]{2,1,0:T(8,128)}), f32[8,8,128]{2,1,0:T(8,128)S(1)}, u32[]{:S(2)}, u32[]{:S(2)}) %all-to-all-start) | async-done | bytes 32800 | tf_op jit(solution)/shard_map/all_to_all | solution.py:448
  16.6 0.0 copy-done.1
  16.6 0.0 copy-done.5
  16.6 0.0 copy-done.10
  16.6 0.0 copy-done.9
  16.6 0.0 copy-done.4
  16.6 0.0 copy-done.3
  16.7 0.0 copy-done.2
  16.7 0.0 copy-start
  16.7 1.1 %copy-done = f32[5,256,128]{2,1,0:T(8,128)S(1)} copy-done((f32[5,256,128]{2,1,0:T(8,128)S(1)}, f32[5,256,128]{2,1,0:T(8,128)}, u32[]{:S(2)}) %copy-start) | copy-done | bytes 655384
  17.8 5.2 %rest.1 = (bf16[1024,128]{1,0:T(8,128)(2,1)}, f32[1024,128]{1,0:T(8,128)S(1)}, bf16[288,128]{1,0:T(8,128)(2,1)S(1)}, f32[24,128]{1,0:T(8,128)S(1)}) custom-call(s32[56]{0:T(128)S(1)} %copy-done.9, s32[56]{0:T(128)S(1)} %copy-done.10, s32[1]{0:T(128)S(6)} %copy.18.count_hbm.count_ref, s32[16]{0:T(128)S(1)} %bitcast.8, ...), custom_call_target="tpu_custom_call" | custom-call | tf_op jit(solution)/shard_map/rest/pallas_call | solution.py:403
  22.9 0.1 collective-permute-start
  23.0 8.0 %collective-permute-start.1 = (bf16[288,128]{1,0:T(8,128)(2,1)S(1)}, bf16[288,128]{1,0:T(8,128)(2,1)S(1)}, u32[]{:S(2)}, u32[]{:S(2)}) collective-permute-start(bf16[288,128]{1,0:T(8,128)(2,1)S(1)} %get-tuple-element.18.sent_ref), channel_id=1, source_target_pairs={{0,8},{2,10},{4,12},{6,14},{8,0},{10,2},{12,4},{14,6},{1,9},{3,11}... | collective-permute-start | bytes 221192 | tf_op jit(solution)/shard_map/ppermute | solution.py:502
  31.0 2.9 %collective-permute-done.1.got_ref = bf16[288,128]{1,0:T(8,128)(2,1)S(1)} collective-permute-done((bf16[288,128]{1,0:T(8,128)(2,1)S(1)}, bf16[288,128]{1,0:T(8,128)(2,1)S(1)}, u32[]{:S(2)}, u32[]{:S(2)}) %collective-permute-start.1) | collective-permute-done | bytes 73760 | tf_op jit(solution)/shard_map/ppermute | solution.py:502
  33.9 0.1 collective-permute-start.2
  33.9 4.3 %collective-permute-done.2.got_ref = bf16[288,128]{1,0:T(8,128)(2,1)S(1)} collective-permute-done((bf16[288,128]{1,0:T(8,128)(2,1)S(1)}, bf16[288,128]{1,0:T(8,128)(2,1)S(1)}, u32[]{:S(2)}, u32[]{:S(2)}) %collective-permute-start.2) | collective-permute-done | bytes 73760 | tf_op jit(solution)/shard_map/ppermute | solution.py:502
  38.3 0.1 collective-permute-start.3
  38.4 4.3 %collective-permute-done.3.got_ref = bf16[272,128]{1,0:T(8,128)(2,1)S(1)} collective-permute-done((bf16[272,128]{1,0:T(8,128)(2,1)S(1)}, bf16[272,128]{1,0:T(8,128)(2,1)S(1)}, u32[]{:S(2)}, u32[]{:S(2)}) %collective-permute-start.3) | collective-permute-done | bytes 69664 | tf_op jit(solution)/shard_map/ppermute | solution.py:502
  42.7 0.0 collective-permute-start.4
  42.7 0.8 %weights.1 = (f32[128,128]{1,0:T(8,128)}, f32[128,128]{1,0:T(8,128)}, f32[1,128]{1,0:T(1,128)}) custom-call(bf16[272,128]{1,0:T(8,128)(2,1)S(1)} %get-tuple-element.22.sent_ref, bf16[272,128]{1,0:T(8,128)(2,1)S(1)} %collective-permute-done.3.got_ref), custom_call_target="tpu_custom_call" | custom-call | tf_op jit(solution)/shard_map/weights/pallas_call | solution.py:403
  43.4 0.4 collective-permute-done.4.other_rows_ref
  43.9 0.0 collective-permute-done.other_partial_ref
  43.9 0.0 copy-done.6
  43.9 0.0 copy-done.7
  43.9 0.0 copy-done.8
  43.9 1.6 %features.1 = bf16[1024,128]{1,0:T(8,128)(2,1)} custom-call(s32[2,8]{1,0:T(2,128)S(1)} %bitcast.11, s32[8]{0:T(128)S(1)} %bitcast.13, s32[16]{0:T(128)S(1)} %bitcast.9, s32[16]{0:T(128)S(1)} %copy-done.8, f32[1024,128]{1,0:T(8,128)S(1)} %get-tuple-element.17.partial_ref, f32[1024,128]{1,0:T(8,128)S(1)} %collective-permute-done.other_partial_ref, ...), custom_call_target="tpu_custom_call" | custom-call | tf_op jit(solution)/shard_map/features/pallas_call | solution.py:403
  (3 shorter events, 0.1 us)
Async XLA Ops:
  0.6 16.0 %copy-start.1 = (bf16[1024,128]{1,0:T(8,128)(2,1)S(1)}, bf16[1024,128]{1,0:T(8,128)(2,1)}, u32[]{:S(2)}) copy-start(bf16[1024,128]{1,0:T(8,128)(2,1)} %features_ref.1) | copy-start | bytes 786436
  0.6 16.0 %copy-start.5 = (s32[16,1]{0,1:T(1,128)S(1)}, s32[16,1]{0,1:T(1,128)}, u32[]{:S(2)}) copy-start(s32[16,1]{0,1:T(1,128)} %param.24) | copy-start | bytes 196
  0.7 16.0 %copy-start.10 = (s32[56]{0:T(128)S(1)}, s32[56]{0:T(128)}, u32[]{:S(2)}) copy-start(s32[56]{0:T(128)} %src_ref.1) | copy-start | bytes 676
  0.7 16.0 %copy-start.9 = (s32[56]{0:T(128)S(1)}, s32[56]{0:T(128)}, u32[]{:S(2)}) copy-start(s32[56]{0:T(128)} %dst_ref.1) | copy-start | bytes 676
  0.7 16.0 %copy-start.4 = (bf16[128,128]{1,0:T(8,128)(2,1)S(1)}, bf16[128,128]{1,0:T(8,128)(2,1)}, u32[]{:S(2)}) copy-start(bf16[128,128]{1,0:T(8,128)(2,1)} %w_neigh_ref.1) | copy-start | bytes 98308
  0.7 16.0 %copy-start.3 = (bf16[128,128]{1,0:T(8,128)(2,1)S(1)}, bf16[128,128]{1,0:T(8,128)(2,1)}, u32[]{:S(2)}) copy-start(bf16[128,128]{1,0:T(8,128)(2,1)} %w_self_ref.1) | copy-start | bytes 98308
  0.7 16.0 %copy-start.2 = (bf16[1024,128]{1,0:T(8,128)(2,1)S(1)}, bf16[1024,128]{1,0:T(8,128)(2,1)}, u32[]{:S(2)}) copy-start(bf16[1024,128]{1,0:T(8,128)(2,1)} %cotangent_ref.1) | copy-start | bytes 786436
  2.7 14.0 %all-to-all-start = ((f32[8,8,128]{2,1,0:T(8,128)}), f32[8,8,128]{2,1,0:T(8,128)S(1)}, u32[]{:S(2)}, u32[]{:S(2)}) async-start(f32[8,8,128]{2,1,0:T(8,128)} %gather.1), calls=%async_computation | async-start | bytes 65536 | tf_op jit(solution)/shard_map/all_to_all | solution.py:448
  10.6 33.3 %copy-start.6 = (s32[1,8,2]{1,2,0:T(2,128)S(1)}, s32[1,8,2]{1,2,0:T(2,128)}, u32[]{:S(2)}) copy-start(s32[1,8,2]{1,2,0:T(2,128)} %param.22) | copy-start | bytes 196
  10.6 33.3 %copy-start.7 = (s32[1,8]{1,0:T(1,128)S(1)}, s32[1,8]{1,0:T(1,128)}, u32[]{:S(2)}) copy-start(s32[1,8]{1,0:T(1,128)} %param.23) | copy-start | bytes 100
  10.6 33.3 %copy-start.8 = (s32[16]{0:T(128)S(1)}, s32[16]{0:T(128)}, u32[]{:S(2)}) copy-start(s32[16]{0:T(128)} %hub_row_ref.1) | copy-start | bytes 196
  16.7 1.1 %copy-start = (f32[5,256,128]{2,1,0:T(8,128)S(1)}, f32[5,256,128]{2,1,0:T(8,128)}, u32[]{:S(2)}) copy-start(f32[5,256,128]{2,1,0:T(8,128)} %own_tiles.1.total_hbm) | copy-start | bytes 1966084
  22.9 20.9 %collective-permute-start = (f32[1024,128]{1,0:T(8,128)S(1)}, f32[1024,128]{1,0:T(8,128)S(1)}, u32[]{:S(2)}, u32[]{:S(2)}) collective-permute-start(f32[1024,128]{1,0:T(8,128)S(1)} %get-tuple-element.17.partial_ref), channel_id=1, source_target_pairs={{0,1},{1,0},{2,3},{3,2},{4,5},{5,4},{6,7},{7,6},{8,9},{9,8},{10,11... | collective-permute-start | bytes 1572872 | tf_op jit(solution)/shard_map/ppermute | solution.py:500
  23.0 10.8 %collective-permute-start.1 = (bf16[288,128]{1,0:T(8,128)(2,1)S(1)}, bf16[288,128]{1,0:T(8,128)(2,1)S(1)}, u32[]{:S(2)}, u32[]{:S(2)}) collective-permute-start(bf16[288,128]{1,0:T(8,128)(2,1)S(1)} %get-tuple-element.18.sent_ref), channel_id=1, source_target_pairs={{0,8},{2,10},{4,12},{6,14},{8,0},{10,2},{12,4},{14,6},{1,9},{3,11}... | collective-permute-start | bytes 221192 | tf_op jit(solution)/shard_map/ppermute | solution.py:502
  33.9 4.4 %collective-permute-start.2 = (bf16[288,128]{1,0:T(8,128)(2,1)S(1)}, bf16[288,128]{1,0:T(8,128)(2,1)S(1)}, u32[]{:S(2)}, u32[]{:S(2)}) collective-permute-start(bf16[288,128]{1,0:T(8,128)(2,1)S(1)} %get-tuple-element.20.sent_ref), channel_id=1, source_target_pairs={{0,4},{2,6},{4,0},{6,2},{8,12},{10,14},{12,8},{14,10},{1,5},{3,7},... | collective-permute-start | bytes 221192 | tf_op jit(solution)/shard_map/ppermute | solution.py:502
  38.3 4.4 %collective-permute-start.3 = (bf16[272,128]{1,0:T(8,128)(2,1)S(1)}, bf16[272,128]{1,0:T(8,128)(2,1)S(1)}, u32[]{:S(2)}, u32[]{:S(2)}) collective-permute-start(bf16[272,128]{1,0:T(8,128)(2,1)S(1)} %get-tuple-element.22.sent_ref), channel_id=1, source_target_pairs={{0,2},{2,0},{4,6},{6,4},{8,10},{10,8},{12,14},{14,12},{1,3},{3,1},... | collective-permute-start | bytes 208904 | tf_op jit(solution)/shard_map/ppermute | solution.py:502
  42.7 1.2 %collective-permute-start.4 = (f32[20,128]{1,0:T(8,128)S(1)}, f32[20,128]{1,0:T(8,128)S(1)}, u32[]{:S(2)}, u32[]{:S(2)}) collective-permute-start(f32[20,128]{1,0:T(8,128)S(1)} %returned.1.own_rows_ref), channel_id=1, source_target_pairs={{0,1},{1,0},{2,3},{3,2},{4,5},{5,4},{6,7},{7,6},{8,9},{9,8},{10,11... | collective-permute-start | bytes 30728 | tf_op jit(solution)/shard_map/ppermute | solution.py:515

commit v3 on v2

--- a/solution.py
+++ b/solution.py
@@ -116,12 +116,16 @@
 
 
 class Tiles:
-    def __init__(self, list_ref, total, source, held, sems):
+    def __init__(self, list_ref, total, source, held, sems, columns=None):
         self.list_ref, self.total, self.source, self.held, self.sems = list_ref, total, source, held, sems
+        self.columns = held.shape[2] if columns is None else columns
 
     def copy(self, position):
         tile = self.list_ref[0, position]
-        return pltpu.make_async_copy(self.source.at[tile], self.held.at[tile], self.sems.at[tile])
+        span = slice(0, self.columns)
+        return pltpu.make_async_copy(
+            self.source.at[tile, :, span], self.held.at[tile, :, span], self.sems.at[tile]
+        )
 
     def start(self):
         def one(position, carry):
@@ -130,15 +134,14 @@
 
         lax.fori_loop(0, self.total, one, 0)
 
-    def each(self, body, wait):
+    def each(self, body):
         def group(step, carry):
-            if wait:
-                for k in range(GROUP_TILES):
-                    position = step * GROUP_TILES + k
-
-                    @pl.when(position < self.total)
-                    def _(position=position):
-                        self.copy(position).wait()
+            for k in range(GROUP_TILES):
+                position = step * GROUP_TILES + k
+
+                @pl.when(position < self.total)
+                def _(position=position):
+                    self.copy(position).wait()
 
             for k in range(GROUP_TILES):
                 position = step * GROUP_TILES + k
@@ -151,12 +154,13 @@
 
 def own_kernel(
     dst_hbm, src_hbm, count_hbm, features_hbm, w_self_hbm, w_neigh_hbm, bias_hbm, adjacency_hbm,
-    total_ref,
+    total_hbm, far_hbm,
     dst_ref, src_ref, count_ref, features_ref, w_self_ref, w_neigh_ref, bias_ref,
-    adjacency_ref, blocks_ref, list_ref, far_list_ref, sems, tile_sems,
+    adjacency_ref, blocks_ref, total_ref, sums_ref, far_ref, list_ref, far_list_ref, sems, tile_sems, out_sems,
 ):
     tile_rows = adjacency_ref.shape[1]
     dst_blocks = total_ref.shape[0] - 1
+    far_blocks, columns = sums_ref.shape[1], sums_ref.shape[3]
     copies = fetch(
         [
             (src_hbm, src_ref), (dst_hbm, dst_ref), (count_hbm, count_ref), (w_neigh_hbm, w_neigh_ref),
@@ -164,12 +168,15 @@
         ],
         sems,
     )
+    sums_ref[...] = jnp.zeros_like(sums_ref)
     for copy in copies[:3]:
         copy.wait()
-    used, _ = split_tiles(list_ref, far_list_ref, dst_ref, src_ref, count_ref[0], dst_blocks)
-    pad_list(list_ref, used, dst_blocks, dst_blocks)
-    tiles = Tiles(list_ref, used, adjacency_hbm, adjacency_ref, tile_sems)
-    tiles.start()
+    near_used, far_used = split_tiles(list_ref, far_list_ref, dst_ref, src_ref, count_ref[0], dst_blocks)
+    far = Tiles(far_list_ref, far_used, adjacency_hbm, adjacency_ref, tile_sems, columns)
+    far.start()
+    near = Tiles(list_ref, near_used, adjacency_hbm, adjacency_ref, tile_sems)
+    near.start()
+    pad_list(list_ref, near_used, dst_blocks, dst_blocks)
     for copy in copies[3:]:
         copy.wait()
     features = features_ref[...]
@@ -182,37 +189,61 @@
         total_ref[block] = base[block * tile_rows : (block + 1) * tile_rows]
     total_ref[dst_blocks] = jnp.zeros(total_ref.shape[1:], F32)
 
+    def add_far(position, carry):
+        far.copy(position).wait()
+        tile = adjacency_ref[far_list_ref[0, position], :, :columns]
+        sums_ref[far_list_ref[1, position], far_list_ref[2, position] - dst_blocks] += tile.astype(F32)
+        return carry
+
+    lax.fori_loop(0, far_used, add_far, 0)
+    for dst in range(dst_blocks):
+        for block in range(far_blocks):
+            far_ref[dst, :, block * columns : (block + 1) * columns] = sums_ref[dst, block].astype(BF16)
+    far_out = pltpu.make_async_copy(far_ref, far_hbm.at[0:dst_blocks], out_sems.at[0])
+    far_out.start()
+
     def forward(tile, dst, src):
         total_ref[dst] += dot(tile, blocks_ref[src])
 
-    tiles.each(forward, wait=True)
+    near.each(forward)
+    total_out = pltpu.make_async_copy(total_ref.at[0:dst_blocks], total_hbm.at[0:dst_blocks], out_sems.at[1])
+    total_out.start()
+    far_out.wait()
+    total_out.wait()
 
 
 def rest_kernel(
     dst_ref, src_ref, count_ref, owner_ref,
-    arrived_ref, total_hbm, features_ref, w_self_ref, w_neigh_ref, cotangent_ref, adjacency_hbm,
-    output_ref, partial_ref, message_ref, keep_ref,
-    halo_ref, hubs_ref, total_ref, rows_ref, low_rows_ref, blocks_ref, grad_ref, grad_t_ref, source_t_ref, back_ref,
-    adjacency_ref, far_list_ref, own_list_ref, counter_ref, tile_sems, total_sem,
-    *, partitions, slots,
+    arrived_ref, total_hbm, far_hbm, features_ref, w_self_ref, w_neigh_ref, cotangent_ref, adjacency_hbm,
+    output_hbm, partial_ref, message_ref, keep_ref,
+    halo_ref, hubs_ref, output_ref, total_ref, far_ref, rows_ref, low_rows_ref, grad_ref, grad_t_ref, source_t_ref,
+    back_ref, adjacency_ref, list_ref, counter_ref, tile_sems, sems,
+    *, partitions, slots, columns,
 ):
     me = lax.axis_index("dom")
     tile_rows = adjacency_ref.shape[1]
-    dst_blocks = total_hbm.shape[0] - 1
+    dst_blocks = total_ref.shape[0]
     halo_blocks = -(-partitions * slots // tile_rows)
-    hub_blocks = -(-owner_ref.shape[0] // tile_rows)
-    extra_blocks = halo_blocks + hub_blocks
-    hub_base = halo_blocks * tile_rows
-    source_blocks = dst_blocks + extra_blocks
-    fetch_total = pltpu.make_async_copy(total_hbm, total_ref, total_sem)
-    fetch_total.start()
-    near_used, far_used = split_tiles(own_list_ref, far_list_ref, dst_ref, src_ref, count_ref[0], dst_blocks)
-    far = Tiles(far_list_ref, far_used, adjacency_hbm, adjacency_ref, tile_sems)
-    far.start()
-    own = Tiles(own_list_ref, near_used, adjacency_hbm, adjacency_ref, tile_sems)
-    own.start()
-    pad_list(far_list_ref, far_used, dst_blocks, source_blocks)
-    pad_list(own_list_ref, near_used, dst_blocks, source_blocks)
+    hub_base = halo_blocks * columns
+    total_in = pltpu.make_async_copy(total_hbm.at[0:dst_blocks], total_ref, sems.at[0])
+    total_in.start()
+    far_in = pltpu.make_async_copy(far_hbm.at[0:dst_blocks], far_ref, sems.at[1])
+    far_in.start()
+
+    def find_near(tile, used):
+        src = src_ref[tile]
+        is_near = src < dst_blocks
+        put(list_ref, used, tile, dst_ref[tile], src)
+
+        @pl.when(is_near)
+        def _():
+            pltpu.make_async_copy(adjacency_hbm.at[tile], adjacency_ref.at[tile], tile_sems.at[tile]).start()
+
+        return used + is_near.astype(jnp.int32)
+
+    used = lax.fori_loop(0, count_ref[0], find_near, jnp.int32(0))
+    near = Tiles(list_ref, used, adjacency_hbm, adjacency_ref, tile_sems)
+    pad_list(list_ref, used, dst_blocks, dst_blocks)
 
     rows_ref[...] = jnp.zeros_like(rows_ref)
 
@@ -226,24 +257,17 @@
         rows_ref[pl.ds(hub_base + hub, 1), :] = arrived_ref[owner, pl.ds(slots + slot, 1), :]
 
     hub_slots(owner_ref, counter_ref, partitions, hub_in)
-    low_rows_ref[...] = rows_ref[...].astype(BF16)
-    for block in range(extra_blocks):
-        rows = low_rows_ref[block * tile_rows : (block + 1) * tile_rows]
-        blocks_ref[block] = dot(rows, w_neigh_ref[...]).astype(BF16)
-    blocks_ref[extra_blocks] = jnp.zeros(blocks_ref.shape[1:], BF16)
-    fetch_total.wait()
-
-    def forward(tile, dst, src):
-        total_ref[dst] += dot(tile, blocks_ref[src - dst_blocks])
-
-    far.each(forward, wait=True)
+    low_rows = rows_ref[...].astype(BF16)
+    low_rows_ref[...] = low_rows
+    far_projected = dot(low_rows, w_neigh_ref[...]).astype(BF16)
+    total_in.wait()
+    far_in.wait()
 
     root = 0.7978845608028654
     bias_sum = jnp.zeros((1, output_ref.shape[1]), F32)
-    w_self_t = jnp.zeros((output_ref.shape[1], features_ref.shape[1]), F32)
     for block in range(dst_blocks):
         span = slice(block * tile_rows, (block + 1) * tile_rows)
-        v = total_ref[block]
+        v = total_ref[block] + dot(far_ref[block], far_projected)
         square = v * v
         gate = jnp.tanh(root * (v + 0.044715 * (v * square)))
         half = 0.5 * (1.0 + gate)
@@ -251,34 +275,32 @@
         slope = half + (0.5 * root) * v * (1.0 - gate * gate) * (1.0 + (3 * 0.044715) * square)
         grad = cotangent_ref[span, :].astype(F32) * slope
         bias_sum += jnp.sum(grad, axis=0, keepdims=True)
-        low = grad.astype(BF16)
-        grad_ref[block] = low
-        low_t = jnp.transpose(grad).astype(BF16)
-        grad_t_ref[block] = low_t
-        w_self_t += dot(low_t, features_ref[span, :])
+        grad_ref[block] = grad.astype(BF16)
+        grad_t_ref[block] = jnp.transpose(grad).astype(BF16)
+    output_out = pltpu.make_async_copy(output_ref, output_hbm, sems.at[2])
+    output_out.start()
     grad_t_ref[dst_blocks] = jnp.zeros(grad_t_ref.shape[1:], BF16)
-
     source_t_ref[...] = jnp.zeros_like(source_t_ref)
 
     def backward(tile, dst, src):
         source_t_ref[src] += dot(grad_t_ref[dst], tile)
 
-    far.each(backward, wait=False)
-    own.each(backward, wait=True)
-
-    w_neigh_t = jnp.zeros_like(w_self_t)
+    near.each(backward)
+
+    far_t = jnp.zeros((output_ref.shape[1], far_ref.shape[2]), F32)
+    for block in range(dst_blocks):
+        far_t += dot(grad_t_ref[block], far_ref[block])
+    back_ref[...] = dot_nt(jnp.transpose(far_t).astype(BF16), w_neigh_ref[...])
+    w_self_t = jnp.zeros((output_ref.shape[1], features_ref.shape[1]), F32)
+    w_neigh_t = dot(far_t.astype(BF16), low_rows_ref[...])
     for block in range(dst_blocks):
         span = slice(block * tile_rows, (block + 1) * tile_rows)
         source_t = source_t_ref[block]
+        w_self_t += dot(grad_t_ref[block], features_ref[span, :])
         w_neigh_t += dot(source_t.astype(BF16), features_ref[span, :])
         partial_ref[span, :] = dot_nt(grad_ref[block], w_self_ref[...]) + dot_nt(
             jnp.transpose(source_t).astype(BF16), w_neigh_ref[...]
         )
-    for block in range(extra_blocks):
-        span = slice(block * tile_rows, (block + 1) * tile_rows)
-        source_t = source_t_ref[dst_blocks + block]
-        w_neigh_t += dot(source_t.astype(BF16), low_rows_ref[span, :])
-        back_ref[span, :] = dot_nt(jnp.transpose(source_t).astype(BF16), w_neigh_ref[...])
 
     def halo_out(q, carry):
         halo_ref[pl.ds((q ^ me) * slots, slots), :] = back_ref[pl.ds(q * slots, slots), :]
@@ -294,6 +316,7 @@
     plan = Exchange(partitions, slots, 0)
     message_ref[0 : plan.weights, :] = jnp.concatenate([w_self_t, w_neigh_t], axis=0).astype(BF16)
     plan.write(message_ref, keep_ref, halo_ref[...], hubs_ref[...], bias_sum)
+    output_out.wait()
 
 
 class Exchange:
@@ -399,12 +422,12 @@
 HBM = pl.BlockSpec(memory_space=pltpu.HBM)
 
 
-def call(kernel, name, ins, outs, scratch, args, grant, flops=0, size=0):
+def call(kernel, name, ins, outs, scratch, args, grant, flops=0, size=0, out_specs=None):
     return pl.pallas_call(
         kernel,
         out_shape=outs,
         in_specs=ins,
-        out_specs=jax.tree.map(lambda _: VMEM, outs),
+        out_specs=jax.tree.map(lambda _: VMEM, outs) if out_specs is None else out_specs,
         scratch_shapes=scratch,
         compiler_params=pltpu.CompilerParams(vmem_limit_bytes=grant * 1024 * 1024),
         cost_estimate=pl.CostEstimate(flops=flops, bytes_accessed=size, transcendentals=0),
@@ -423,7 +446,8 @@
     slots = send_rows.shape[2]
     hubs = hub_row.shape[0]
     dst_blocks = nodes // tile_rows
-    extra_blocks = -(-partitions * slots // tile_rows) - (-hubs // tile_rows)
+    far_blocks = -(-partitions * slots // tile_rows) - (-hubs // tile_rows)
+    columns = min(tile_rows, -(-max(partitions * slots, hubs) // 128) * 128)
     rows = jnp.transpose(send_rows[0])
     counts = send_count.reshape(partitions)
     owner = hub_owner.reshape(hubs)
@@ -446,9 +470,12 @@
         (rows, counts, owner, hub_row, features), 60,
     )
     arrived = lax.all_to_all(bundle, "dom", split_axis=0, concat_axis=0, tiled=True)
-    total = call(
+    total, far = call(
         own_kernel, "own_tiles", [HBM] * 8,
-        struct((dst_blocks + 1, tile_rows, hidden), F32),
+        (
+            struct((limit, tile_rows, hidden), F32),
+            struct((limit, tile_rows, far_blocks * columns), BF16),
+        ),
         [
             pltpu.SMEM((limit,), jnp.int32),
             pltpu.SMEM((limit,), jnp.int32),
@@ -459,18 +486,22 @@
             pltpu.VMEM((1, hidden), F32),
             pltpu.VMEM(adjacency.shape, BF16),
             pltpu.VMEM((dst_blocks + 1, tile_rows, hidden), BF16),
+            pltpu.VMEM((dst_blocks + 1, tile_rows, hidden), F32),
+            pltpu.VMEM((dst_blocks, far_blocks, tile_rows, columns), F32),
+            pltpu.VMEM((dst_blocks, tile_rows, far_blocks * columns), BF16),
             lists,
             lists,
             pltpu.SemaphoreType.DMA((7,)),
             pltpu.SemaphoreType.DMA((limit,)),
+            pltpu.SemaphoreType.DMA((2,)),
         ],
-        (tile_dst, tile_src, tile_count, features, w_self, w_neigh, bias.reshape(1, hidden), adjacency), 54,
-        flops=2 * limit * tile_rows * tile_rows * hidden, size=adjacency.size * 2,
+        (tile_dst, tile_src, tile_count, features, w_self, w_neigh, bias.reshape(1, hidden), adjacency),
+        54, flops=2 * limit * tile_rows * tile_rows * hidden, size=adjacency.size * 2, out_specs=(HBM, HBM),
     )
     plans = [Exchange(partitions, slots, step) for step in range(partitions.bit_length() - 1)]
     output, partial, message, keep = call(
-        functools.partial(rest_kernel, partitions=partitions, slots=slots), "rest",
-        [SMEM] * 4 + [VMEM, HBM] + [VMEM] * 4 + [HBM],
+        functools.partial(rest_kernel, partitions=partitions, slots=slots, columns=columns), "rest",
+        [SMEM] * 4 + [VMEM, HBM, HBM] + [VMEM] * 4 + [HBM],
         (
             struct((nodes, hidden), BF16),
             struct((nodes, inputs), F32),
@@ -480,22 +511,26 @@
         [
             pltpu.VMEM((partitions * slots, inputs), F32),
             pltpu.VMEM((partitions * HUB_MOST, inputs), F32),
-            pltpu.VMEM((dst_blocks + 1, tile_rows, hidden), F32),
-            pltpu.VMEM((extra_blocks * tile_rows, inputs), F32),
-            pltpu.VMEM((extra_blocks * tile_rows, inputs), BF16),
-            pltpu.VMEM((extra_blocks + 1, tile_rows, hidden), BF16),
+            pltpu.VMEM((nodes, hidden), BF16),
+            pltpu.VMEM((dst_blocks, tile_rows, hidden), F32),
+            pltpu.VMEM((dst_blocks, tile_rows, far_blocks * columns), BF16),
+            pltpu.VMEM((far_blocks * columns, inputs), F32),
+            pltpu.VMEM((far_blocks * columns, inputs), BF16),
             pltpu.VMEM((dst_blocks, tile_rows, hidden), BF16),
             pltpu.VMEM((dst_blocks + 1, hidden, tile_rows), BF16),
-            pltpu.VMEM((dst_blocks + extra_blocks + 1, hidden, tile_rows), F32),
-            pltpu.VMEM((extra_blocks * tile_rows, inputs), F32),
+            pltpu.VMEM((dst_blocks + 1, hidden, tile_rows), F32),
+            pltpu.VMEM((far_blocks * columns, inputs), F32),
             pltpu.VMEM(adjacency.shape, BF16),
-            lists,
             lists,
             pltpu.SMEM((partitions,), jnp.int32),
             pltpu.SemaphoreType.DMA((limit,)),
-            pltpu.SemaphoreType.DMA,
+            pltpu.SemaphoreType.DMA((3,)),
         ],
-        (tile_dst, tile_src, tile_count, owner, arrived, total, features, w_self, w_neigh, cotangent, adjacency), 50,
+        (
+            tile_dst, tile_src, tile_count, owner,
+            arrived, total, far, features, w_self, w_neigh, cotangent, adjacency,
+        ),
+        50, out_specs=(HBM, VMEM, VMEM, VMEM),
     )
     other_partial = lax.ppermute(partial, "feat", [(0, 1), (1, 0)])
     for now in plans:

time: 45.5 us -> 40.9 us (0.90)
  starting transfers between devices: 15.4 us -> 12.8 us
  Pallas kernels: 13.2 us -> 12.1 us
  local copies, waits for them, and re-layouts: 1.14 us -> 0.06 us
    ppermute x3, starting transfers between devices: 8.1 us -> 5.49 us  [local(): lax.ppermute(message, 'dom', [(q, q ^ now.half) for q in range(partitions)])]
    pallas_call x8, Pallas kernels: 13.2 us -> 12.1 us  [call(): pl.pallas_call(kernel, out_shape=outs, in_specs=ins, out_specs=jax.tree.m...]
    unnamed x22 -> x20, local copies, waits for them, and re-layouts: 1.14 us -> 0.06 us
  transfers between devices with their start and end apart: 6 -> 6, of which waited for: 5 -> 5; matrix products, arithmetic and copies ran while one was open for 0% -> 0% of each run, Pallas kernels for 10% -> 11%
where the time goes in v3:
time: 40.9 us; the launch traced here: 40.7 us
  waiting for transfers between devices  14.3 us (35%)
  starting transfers between devices  12.8 us (31%)
  Pallas kernels  12.1 us (30%)
  between operations  1.46 us (4%)
    pallas_call x8, Pallas kernels, call(): pl.pallas_call(kernel, out_shape=outs, in_specs=ins, out_specs=jax.tree.m...  12.1 us
    ppermute x3, waiting for transfers between devices, local(): lax.ppermute(message, 'dom', [(q, q ^ now.half) for q in range(partitions)])  11.5 us
    all_to_all x1, starting transfers between devices, local(): lax.all_to_all(bundle, 'dom', split_axis=0, concat_axis=0, tiled=True)  7.27 us
    ppermute x3, starting transfers between devices, local(): lax.ppermute(message, 'dom', [(q, q ^ now.half) for q in range(partitions)])  5.49 us
    all_to_all x1, waiting for transfers between devices, local(): lax.all_to_all(bundle, 'dom', split_axis=0, concat_axis=0, tiled=True)  2.34 us
  transfers between devices with their start and end apart: 6, of which 5 were waited for; matrix products, arithmetic and copies ran while one was open for 0% of the time, Pallas kernels for 11%

profile of v3, /device:TPU:0, one launch (start us, length us, event | category | flops | bytes accessed | tf_op | source)
XLA Modules:
  0.0 40.7 jit_solution(8705822075475867932)
XLA Ops:
  0.6 0.0 copy-start
  0.6 0.0 copy-start.4
  0.7 0.0 copy-start.9
  0.7 0.0 copy-start.8
  0.7 0.0 copy-start.3
  0.7 0.0 copy-start.2
  0.7 0.0 copy-start.1
  0.7 1.9 %gather.1 = f32[8,8,128]{2,1,0:T(8,128)} custom-call(s32[2,8]{1,0:T(2,128)} %bitcast.10, s32[8]{0:T(128)} %bitcast.12, s32[16]{0:T(128)} %bitcast.7, s32[16]{0:T(128)} %hub_row_ref.1, bf16[1024,128]{1,0:T(8,128)(2,1)} %features_ref.1), custom_call_target="tpu_custom_call" | custom-call | tf_op jit(solution)/shard_map/gather/pallas_call | solution.py:426
  2.7 7.3 %all-to-all-start = ((f32[8,8,128]{2,1,0:T(8,128)}), f32[8,8,128]{2,1,0:T(8,128)S(1)}, u32[]{:S(2)}, u32[]{:S(2)}) async-start(f32[8,8,128]{2,1,0:T(8,128)} %gather.1), calls=%async_computation | async-start | bytes 65536 | tf_op jit(solution)/shard_map/all_to_all | solution.py:472
  10.6 3.7 %own_tiles.1 = (f32[56,256,128]{2,1,0:T(8,128)}, bf16[56,256,256]{2,1,0:T(8,128)(2,1)}) custom-call(s32[56]{0:T(128)} %dst_ref.1, s32[56]{0:T(128)} %src_ref.1, s32[1]{0:T(128)S(6)} %copy.18.count_hbm.count_ref, bf16[1024,128]{1,0:T(8,128)(2,1)} %features_ref.1, bf16[128,128]{1,0:T(8,128)(2,1)} %w_self_ref.1, bf16[128,128]{1,0:T(8,128)(2,1)} %w_neigh_ref.1, ...), custom_call_target="tpu_custom_call" | custom-call | flops 939524096 | bytes 7340032 | tf_op jit(solution)/shard_map/own_tiles/pallas_call | solution.py:426
  14.3 2.3 %all-to-all-done.arrived_ref = f32[8,8,128]{2,1,0:T(8,128)S(1)} async-done(((f32[8,8,128]{2,1,0:T(8,128)}), f32[8,8,128]{2,1,0:T(8,128)S(1)}, u32[]{:S(2)}, u32[]{:S(2)}) %all-to-all-start) | async-done | bytes 32800 | tf_op jit(solution)/shard_map/all_to_all | solution.py:472
  16.6 0.0 copy-done
  16.6 0.0 copy-done.4
  16.6 0.0 copy-done.9
  16.6 0.0 copy-done.8
  16.6 0.0 copy-done.3
  16.6 0.0 copy-done.2
  16.7 0.0 copy-done.1
  16.7 0.0 copy-start.5
  16.7 0.0 copy-start.6
  16.7 0.0 copy-start.7
  16.7 4.1 %rest.1 = (bf16[1024,128]{1,0:T(8,128)(2,1)}, f32[1024,128]{1,0:T(8,128)S(1)}, bf16[288,128]{1,0:T(8,128)(2,1)S(1)}, f32[24,128]{1,0:T(8,128)S(1)}) custom-call(s32[56]{0:T(128)S(1)} %copy-done.8, s32[56]{0:T(128)S(1)} %copy-done.9, s32[1]{0:T(128)S(6)} %copy.18.count_hbm.count_ref, s32[16]{0:T(128)S(1)} %bitcast.8, ...), custom_call_target="tpu_custom_call" | custom-call | tf_op jit(solution)/shard_map/rest/pallas_call | solution.py:426
  20.8 0.1 collective-permute-start
  20.9 5.3 %collective-permute-start.1 = (bf16[288,128]{1,0:T(8,128)(2,1)S(1)}, bf16[288,128]{1,0:T(8,128)(2,1)S(1)}, u32[]{:S(2)}, u32[]{:S(2)}) collective-permute-start(bf16[288,128]{1,0:T(8,128)(2,1)S(1)} %get-tuple-element.22.sent_ref), channel_id=1, source_target_pairs={{0,8},{2,10},{4,12},{6,14},{8,0},{10,2},{12,4},{14,6},{1,9},{3,11}... | collective-permute-start | bytes 221192 | tf_op jit(solution)/shard_map/ppermute | solution.py:537
  26.2 2.9 %collective-permute-done.1.got_ref = bf16[288,128]{1,0:T(8,128)(2,1)S(1)} collective-permute-done((bf16[288,128]{1,0:T(8,128)(2,1)S(1)}, bf16[288,128]{1,0:T(8,128)(2,1)S(1)}, u32[]{:S(2)}, u32[]{:S(2)}) %collective-permute-start.1) | collective-permute-done | bytes 73760 | tf_op jit(solution)/shard_map/ppermute | solution.py:537
  29.1 0.1 collective-permute-start.2
  29.2 4.3 %collective-permute-done.2.got_ref = bf16[288,128]{1,0:T(8,128)(2,1)S(1)} collective-permute-done((bf16[288,128]{1,0:T(8,128)(2,1)S(1)}, bf16[288,128]{1,0:T(8,128)(2,1)S(1)}, u32[]{:S(2)}, u32[]{:S(2)}) %collective-permute-start.2) | collective-permute-done | bytes 73760 | tf_op jit(solution)/shard_map/ppermute | solution.py:537
  33.6 0.1 collective-permute-start.3
  33.6 4.3 %collective-permute-done.3.got_ref = bf16[272,128]{1,0:T(8,128)(2,1)S(1)} collective-permute-done((bf16[272,128]{1,0:T(8,128)(2,1)S(1)}, bf16[272,128]{1,0:T(8,128)(2,1)S(1)}, u32[]{:S(2)}, u32[]{:S(2)}) %collective-permute-start.3) | collective-permute-done | bytes 69664 | tf_op jit(solution)/shard_map/ppermute | solution.py:537
  37.9 0.0 collective-permute-start.4
  37.9 0.8 %weights.1 = (f32[128,128]{1,0:T(8,128)}, f32[128,128]{1,0:T(8,128)}, f32[1,128]{1,0:T(1,128)}) custom-call(bf16[272,128]{1,0:T(8,128)(2,1)S(1)} %get-tuple-element.26.sent_ref, bf16[272,128]{1,0:T(8,128)(2,1)S(1)} %collective-permute-done.3.got_ref), custom_call_target="tpu_custom_call" | custom-call | tf_op jit(solution)/shard_map/weights/pallas_call | solution.py:426
  38.7 0.4 %collective-permute-done.4.other_rows_ref = f32[20,128]{1,0:T(8,128)S(1)} collective-permute-done((f32[20,128]{1,0:T(8,128)S(1)}, f32[20,128]{1,0:T(8,128)S(1)}, u32[]{:S(2)}, u32[]{:S(2)}) %collective-permute-start.4) | collective-permute-done | bytes 10272 | tf_op jit(solution)/shard_map/ppermute | solution.py:550
  39.1 0.0 collective-permute-done.other_partial_ref
  39.1 0.0 copy-done.5
  39.1 0.0 copy-done.6
  39.1 0.0 copy-done.7
  39.1 1.6 %features.1 = bf16[1024,128]{1,0:T(8,128)(2,1)} custom-call(s32[2,8]{1,0:T(2,128)S(1)} %bitcast.11, s32[8]{0:T(128)S(1)} %bitcast.13, s32[16]{0:T(128)S(1)} %bitcast.9, s32[16]{0:T(128)S(1)} %copy-done.7, f32[1024,128]{1,0:T(8,128)S(1)} %get-tuple-element.21.partial_ref, f32[1024,128]{1,0:T(8,128)S(1)} %collective-permute-done.other_partial_ref, ...), custom_call_target="tpu_custom_call" | custom-call | tf_op jit(solution)/shard_map/features/pallas_call | solution.py:426
  (3 shorter events, 0.1 us)
Async XLA Ops:
  0.6 16.0 %copy-start = (bf16[1024,128]{1,0:T(8,128)(2,1)S(1)}, bf16[1024,128]{1,0:T(8,128)(2,1)}, u32[]{:S(2)}) copy-start(bf16[1024,128]{1,0:T(8,128)(2,1)} %features_ref.1) | copy-start | bytes 786436
  0.6 16.0 %copy-start.4 = (s32[16,1]{0,1:T(1,128)S(1)}, s32[16,1]{0,1:T(1,128)}, u32[]{:S(2)}) copy-start(s32[16,1]{0,1:T(1,128)} %param.24) | copy-start | bytes 196
  0.7 16.0 %copy-start.9 = (s32[56]{0:T(128)S(1)}, s32[56]{0:T(128)}, u32[]{:S(2)}) copy-start(s32[56]{0:T(128)} %src_ref.1) | copy-start | bytes 676
  0.7 16.0 %copy-start.8 = (s32[56]{0:T(128)S(1)}, s32[56]{0:T(128)}, u32[]{:S(2)}) copy-start(s32[56]{0:T(128)} %dst_ref.1) | copy-start | bytes 676
  0.7 16.0 %copy-start.3 = (bf16[128,128]{1,0:T(8,128)(2,1)S(1)}, bf16[128,128]{1,0:T(8,128)(2,1)}, u32[]{:S(2)}) copy-start(bf16[128,128]{1,0:T(8,128)(2,1)} %w_neigh_ref.1) | copy-start | bytes 98308
  0.7 16.0 %copy-start.2 = (bf16[128,128]{1,0:T(8,128)(2,1)S(1)}, bf16[128,128]{1,0:T(8,128)(2,1)}, u32[]{:S(2)}) copy-start(bf16[128,128]{1,0:T(8,128)(2,1)} %w_self_ref.1) | copy-start | bytes 98308
  0.7 16.0 %copy-start.1 = (bf16[1024,128]{1,0:T(8,128)(2,1)S(1)}, bf16[1024,128]{1,0:T(8,128)(2,1)}, u32[]{:S(2)}) copy-start(bf16[1024,128]{1,0:T(8,128)(2,1)} %cotangent_ref.1) | copy-start | bytes 786436
  2.7 14.0 %all-to-all-start = ((f32[8,8,128]{2,1,0:T(8,128)}), f32[8,8,128]{2,1,0:T(8,128)S(1)}, u32[]{:S(2)}, u32[]{:S(2)}) async-start(f32[8,8,128]{2,1,0:T(8,128)} %gather.1), calls=%async_computation | async-start | bytes 65536 | tf_op jit(solution)/shard_map/all_to_all | solution.py:472
  16.7 22.5 %copy-start.5 = (s32[1,8,2]{1,2,0:T(2,128)S(1)}, s32[1,8,2]{1,2,0:T(2,128)}, u32[]{:S(2)}) copy-start(s32[1,8,2]{1,2,0:T(2,128)} %param.22) | copy-start | bytes 196
  16.7 22.5 %copy-start.6 = (s32[1,8]{1,0:T(1,128)S(1)}, s32[1,8]{1,0:T(1,128)}, u32[]{:S(2)}) copy-start(s32[1,8]{1,0:T(1,128)} %param.23) | copy-start | bytes 100
  16.7 22.4 %copy-start.7 = (s32[16]{0:T(128)S(1)}, s32[16]{0:T(128)}, u32[]{:S(2)}) copy-start(s32[16]{0:T(128)} %hub_row_ref.1) | copy-start | bytes 196
  20.8 18.3 %collective-permute-start = (f32[1024,128]{1,0:T(8,128)S(1)}, f32[1024,128]{1,0:T(8,128)S(1)}, u32[]{:S(2)}, u32[]{:S(2)}) collective-permute-start(f32[1024,128]{1,0:T(8,128)S(1)} %get-tuple-element.21.partial_ref), channel_id=1, source_target_pairs={{0,1},{1,0},{2,3},{3,2},{4,5},{5,4},{6,7},{7,6},{8,9},{9,8},{10,11... | collective-permute-start | bytes 1572872 | tf_op jit(solution)/shard_map/ppermute | solution.py:535
  20.9 8.2 %collective-permute-start.1 = (bf16[288,128]{1,0:T(8,128)(2,1)S(1)}, bf16[288,128]{1,0:T(8,128)(2,1)S(1)}, u32[]{:S(2)}, u32[]{:S(2)}) collective-permute-start(bf16[288,128]{1,0:T(8,128)(2,1)S(1)} %get-tuple-element.22.sent_ref), channel_id=1, source_target_pairs={{0,8},{2,10},{4,12},{6,14},{8,0},{10,2},{12,4},{14,6},{1,9},{3,11}... | collective-permute-start | bytes 221192 | tf_op jit(solution)/shard_map/ppermute | solution.py:537
  29.1 4.4 %collective-permute-start.2 = (bf16[288,128]{1,0:T(8,128)(2,1)S(1)}, bf16[288,128]{1,0:T(8,128)(2,1)S(1)}, u32[]{:S(2)}, u32[]{:S(2)}) collective-permute-start(bf16[288,128]{1,0:T(8,128)(2,1)S(1)} %get-tuple-element.24.sent_ref), channel_id=1, source_target_pairs={{0,4},{2,6},{4,0},{6,2},{8,12},{10,14},{12,8},{14,10},{1,5},{3,7},... | collective-permute-start | bytes 221192 | tf_op jit(solution)/shard_map/ppermute | solution.py:537
  33.6 4.4 %collective-permute-start.3 = (bf16[272,128]{1,0:T(8,128)(2,1)S(1)}, bf16[272,128]{1,0:T(8,128)(2,1)S(1)}, u32[]{:S(2)}, u32[]{:S(2)}) collective-permute-start(bf16[272,128]{1,0:T(8,128)(2,1)S(1)} %get-tuple-element.26.sent_ref), channel_id=1, source_target_pairs={{0,2},{2,0},{4,6},{6,4},{8,10},{10,8},{12,14},{14,12},{1,3},{3,1},... | collective-permute-start | bytes 208904 | tf_op jit(solution)/shard_map/ppermute | solution.py:537
  37.9 1.2 %collective-permute-start.4 = (f32[20,128]{1,0:T(8,128)S(1)}, f32[20,128]{1,0:T(8,128)S(1)}, u32[]{:S(2)}, u32[]{:S(2)}) collective-permute-start(f32[20,128]{1,0:T(8,128)S(1)} %returned.1.own_rows_ref), channel_id=1, source_target_pairs={{0,1},{1,0},{2,3},{3,2},{4,5},{5,4},{6,7},{7,6},{8,9},{9,8},{10,11... | collective-permute-start | bytes 30728 | tf_op jit(solution)/shard_map/ppermute | solution.py:550

commit v4 on v3

--- a/solution.py
+++ b/solution.py
@@ -10,6 +10,7 @@
 HUB_MOST = 4
 PEER_ROWS = 8
 GROUP_TILES = 8
+FAR_GROUP = 4
 F32 = jnp.float32
 BF16 = jnp.bfloat16
 NT = (((1,), (1,)), ((), ()))
@@ -71,13 +72,8 @@
     wide_ref[...] = features_ref[...].astype(F32)
 
     def hub(index, slot):
-        mine = owner_ref[index] == own
-
-        @pl.when(mine)
-        def _():
-            hubs_ref[pl.ds(slots + slot, 1), :] = wide_ref[pl.ds(hub_row_ref[index], 1), :]
-
-        return slot + mine.astype(jnp.int32)
+        hubs_ref[pl.ds(slots + slot, 1), :] = wide_ref[pl.ds(hub_row_ref[index], 1), :]
+        return slot + (owner_ref[index] == own).astype(jnp.int32)
 
     repeat(owner_ref.shape[0], hub, jnp.int32(0))
 
@@ -91,65 +87,48 @@
     repeat(partitions, peer, 0)
 
 
-def put(list_ref, position, tile, dst, src):
-    list_ref[0, position] = tile
-    list_ref[1, position] = dst
-    list_ref[2, position] = src
-
-
-def split_tiles(near_ref, far_ref, dst_ref, src_ref, count, split):
-    def visit(tile, used):
-        src, dst = src_ref[tile], dst_ref[tile]
-        near, far = used
-        put(near_ref, near, tile, dst, src)
-        put(far_ref, far, tile, dst, src)
-        is_near = (src < split).astype(jnp.int32)
-        return near + is_near, far + 1 - is_near
-
-    return lax.fori_loop(0, count, visit, (jnp.int32(0), jnp.int32(0)))
-
-
-def pad_list(list_ref, used, dst, src):
-    first = list_ref[0, 0]
-    for k in range(GROUP_TILES):
-        put(list_ref, used + k, first, dst, src)
+def pack_tile(tile, dst, src):
+    return tile + (dst << 8) + (src << 16)
+
+
+def pad_list(list_ref, used, dst, src, group):
+    spare = pack_tile(list_ref[0] & 255, dst, src)
+    for k in range(group):
+        list_ref[used + k] = spare
 
 
 class Tiles:
-    def __init__(self, list_ref, total, source, held, sems, columns=None):
-        self.list_ref, self.total, self.source, self.held, self.sems = list_ref, total, source, held, sems
+    def __init__(self, list_ref, source, held, sems, columns=None):
+        self.list_ref, self.source, self.held, self.sems = list_ref, source, held, sems
         self.columns = held.shape[2] if columns is None else columns
 
-    def copy(self, position):
-        tile = self.list_ref[0, position]
+    def copy(self, tile):
         span = slice(0, self.columns)
         return pltpu.make_async_copy(
             self.source.at[tile, :, span], self.held.at[tile, :, span], self.sems.at[tile]
         )
 
-    def start(self):
+    def start(self, total):
         def one(position, carry):
-            self.copy(position).start()
+            self.copy(self.list_ref[position] & 255).start()
             return carry
 
-        lax.fori_loop(0, self.total, one, 0)
-
-    def each(self, body):
+        lax.fori_loop(0, total, one, 0)
+
+    def each(self, total, size, body):
         def group(step, carry):
-            for k in range(GROUP_TILES):
-                position = step * GROUP_TILES + k
-
-                @pl.when(position < self.total)
-                def _(position=position):
-                    self.copy(position).wait()
-
-            for k in range(GROUP_TILES):
-                position = step * GROUP_TILES + k
-                tile = self.held[self.list_ref[0, position]]
-                body(tile, self.list_ref[1, position], self.list_ref[2, position])
+            codes = [self.list_ref[step * size + k] for k in range(size)]
+            for k in range(size):
+
+                @pl.when(step * size + k < total)
+                def _(k=k):
+                    self.copy(codes[k] & 255).wait()
+
+            for code in codes:
+                body(code & 255, (code >> 8) & 255, code >> 16)
             return carry
 
-        lax.fori_loop(0, (self.total + GROUP_TILES - 1) // GROUP_TILES, group, 0)
+        lax.fori_loop(0, (total + size - 1) // size, group, 0)
 
 
 def own_kernel(
@@ -171,12 +150,26 @@
     sums_ref[...] = jnp.zeros_like(sums_ref)
     for copy in copies[:3]:
         copy.wait()
-    near_used, far_used = split_tiles(list_ref, far_list_ref, dst_ref, src_ref, count_ref[0], dst_blocks)
-    far = Tiles(far_list_ref, far_used, adjacency_hbm, adjacency_ref, tile_sems, columns)
-    far.start()
-    near = Tiles(list_ref, near_used, adjacency_hbm, adjacency_ref, tile_sems)
-    near.start()
-    pad_list(list_ref, near_used, dst_blocks, dst_blocks)
+    far = Tiles(far_list_ref, adjacency_hbm, adjacency_ref, tile_sems, columns)
+    near = Tiles(list_ref, adjacency_hbm, adjacency_ref, tile_sems)
+
+    def split(tile, used):
+        near_used, far_used = used
+        code = pack_tile(tile, dst_ref[tile], src_ref[tile])
+        list_ref[near_used] = code
+        far_list_ref[far_used] = code
+        is_near = (code < (dst_blocks << 16)).astype(jnp.int32)
+
+        @pl.when(is_near == 0)
+        def _():
+            far.copy(tile).start()
+
+        return near_used + is_near, far_used + 1 - is_near
+
+    near_used, far_used = lax.fori_loop(0, count_ref[0], split, (jnp.int32(0), jnp.int32(0)))
+    near.start(near_used)
+    pad_list(list_ref, near_used, dst_blocks, dst_blocks, GROUP_TILES)
+    pad_list(far_list_ref, far_used, dst_blocks, dst_blocks, FAR_GROUP)
     for copy in copies[3:]:
         copy.wait()
     features = features_ref[...]
@@ -189,13 +182,10 @@
         total_ref[block] = base[block * tile_rows : (block + 1) * tile_rows]
     total_ref[dst_blocks] = jnp.zeros(total_ref.shape[1:], F32)
 
-    def add_far(position, carry):
-        far.copy(position).wait()
-        tile = adjacency_ref[far_list_ref[0, position], :, :columns]
-        sums_ref[far_list_ref[1, position], far_list_ref[2, position] - dst_blocks] += tile.astype(F32)
-        return carry
-
-    lax.fori_loop(0, far_used, add_far, 0)
+    def add_far(tile, dst, src):
+        sums_ref[dst, src - dst_blocks] += adjacency_ref[tile, :, :columns].astype(F32)
+
+    far.each(far_used, FAR_GROUP, add_far)
     for dst in range(dst_blocks):
         for block in range(far_blocks):
             far_ref[dst, :, block * columns : (block + 1) * columns] = sums_ref[dst, block].astype(BF16)
@@ -203,9 +193,9 @@
     far_out.start()
 
     def forward(tile, dst, src):
-        total_ref[dst] += dot(tile, blocks_ref[src])
-
-    near.each(forward)
+        total_ref[dst] += dot(adjacency_ref[tile], blocks_ref[src])
+
+    near.each(near_used, GROUP_TILES, forward)
     total_out = pltpu.make_async_copy(total_ref.at[0:dst_blocks], total_hbm.at[0:dst_blocks], out_sems.at[1])
     total_out.start()
     far_out.wait()
@@ -216,7 +206,7 @@
     dst_ref, src_ref, count_ref, owner_ref,
     arrived_ref, total_hbm, far_hbm, features_ref, w_self_ref, w_neigh_ref, cotangent_ref, adjacency_hbm,
     output_hbm, partial_ref, message_ref, keep_ref,
-    halo_ref, hubs_ref, output_ref, total_ref, far_ref, rows_ref, low_rows_ref, grad_ref, grad_t_ref, source_t_ref,
+    halo_ref, hubs_ref, output_ref, total_ref, far_ref, rows_ref, low_rows_ref, grad_t_ref, source_t_ref,
     back_ref, adjacency_ref, list_ref, counter_ref, tile_sems, sems,
     *, partitions, slots, columns,
 ):
@@ -230,20 +220,21 @@
     far_in = pltpu.make_async_copy(far_hbm.at[0:dst_blocks], far_ref, sems.at[1])
     far_in.start()
 
+    near = Tiles(list_ref, adjacency_hbm, adjacency_ref, tile_sems)
+
     def find_near(tile, used):
-        src = src_ref[tile]
-        is_near = src < dst_blocks
-        put(list_ref, used, tile, dst_ref[tile], src)
+        code = pack_tile(tile, dst_ref[tile], src_ref[tile])
+        list_ref[used] = code
+        is_near = code < (dst_blocks << 16)
 
         @pl.when(is_near)
         def _():
-            pltpu.make_async_copy(adjacency_hbm.at[tile], adjacency_ref.at[tile], tile_sems.at[tile]).start()
+            near.copy(tile).start()
 
         return used + is_near.astype(jnp.int32)
 
     used = lax.fori_loop(0, count_ref[0], find_near, jnp.int32(0))
-    near = Tiles(list_ref, used, adjacency_hbm, adjacency_ref, tile_sems)
-    pad_list(list_ref, used, dst_blocks, dst_blocks)
+    pad_list(list_ref, used, dst_blocks, dst_blocks, GROUP_TILES)
 
     rows_ref[...] = jnp.zeros_like(rows_ref)
 
@@ -265,6 +256,8 @@
 
     root = 0.7978845608028654
     bias_sum = jnp.zeros((1, output_ref.shape[1]), F32)
+    w_self_t = jnp.zeros((output_ref.shape[1], features_ref.shape[1]), F32)
+    far_t = jnp.zeros((output_ref.shape[1], far_ref.shape[2]), F32)
     for block in range(dst_blocks):
         span = slice(block * tile_rows, (block + 1) * tile_rows)
         v = total_ref[block] + dot(far_ref[block], far_projected)
@@ -275,32 +268,28 @@
         slope = half + (0.5 * root) * v * (1.0 - gate * gate) * (1.0 + (3 * 0.044715) * square)
         grad = cotangent_ref[span, :].astype(F32) * slope
         bias_sum += jnp.sum(grad, axis=0, keepdims=True)
-        grad_ref[block] = grad.astype(BF16)
-        grad_t_ref[block] = jnp.transpose(grad).astype(BF16)
+        low_t = jnp.transpose(grad.astype(BF16))
+        grad_t_ref[block] = low_t
+        partial_ref[span, :] = dot_nt(grad.astype(BF16), w_self_ref[...])
+        w_self_t += dot(low_t, features_ref[span, :])
+        far_t += dot(low_t, far_ref[block])
     output_out = pltpu.make_async_copy(output_ref, output_hbm, sems.at[2])
     output_out.start()
     grad_t_ref[dst_blocks] = jnp.zeros(grad_t_ref.shape[1:], BF16)
     source_t_ref[...] = jnp.zeros_like(source_t_ref)
 
     def backward(tile, dst, src):
-        source_t_ref[src] += dot(grad_t_ref[dst], tile)
-
-    near.each(backward)
-
-    far_t = jnp.zeros((output_ref.shape[1], far_ref.shape[2]), F32)
-    for block in range(dst_blocks):
-        far_t += dot(grad_t_ref[block], far_ref[block])
-    back_ref[...] = dot_nt(jnp.transpose(far_t).astype(BF16), w_neigh_ref[...])
-    w_self_t = jnp.zeros((output_ref.shape[1], features_ref.shape[1]), F32)
+        source_t_ref[src] += dot(grad_t_ref[dst], adjacency_ref[tile])
+
+    near.each(used, GROUP_TILES, backward)
+
+    back_ref[...] = dot_nt(jnp.transpose(far_t.astype(BF16)), w_neigh_ref[...])
     w_neigh_t = dot(far_t.astype(BF16), low_rows_ref[...])
     for block in range(dst_blocks):
         span = slice(block * tile_rows, (block + 1) * tile_rows)
-        source_t = source_t_ref[block]
-        w_self_t += dot(grad_t_ref[block], features_ref[span, :])
-        w_neigh_t += dot(source_t.astype(BF16), features_ref[span, :])
-        partial_ref[span, :] = dot_nt(grad_ref[block], w_self_ref[...]) + dot_nt(
-            jnp.transpose(source_t).astype(BF16), w_neigh_ref[...]
-        )
+        source_t = source_t_ref[block].astype(BF16)
+        w_neigh_t += dot(source_t, features_ref[span, :])
+        partial_ref[span, :] += dot_nt(jnp.transpose(source_t), w_neigh_ref[...])
 
     def halo_out(q, carry):
         halo_ref[pl.ds((q ^ me) * slots, slots), :] = back_ref[pl.ds(q * slots, slots), :]
@@ -348,8 +337,10 @@
         parts = halo_send + hub_send + [high, bias - high]
         if spare:
             parts.append(jnp.zeros((spare, bias.shape[1]), F32))
-        message_ref[self.weights : self.rows, :] = jnp.concatenate(parts, axis=0).astype(BF16)
+        sent = jnp.concatenate(parts, axis=0).astype(BF16)
+        message_ref[self.weights : self.rows, :] = sent
         keep_ref[...] = jnp.concatenate(halo_keep + hub_keep, axis=0)
+        return sent
 
     def tail(self, ref):
         return ref[self.weights : self.rows, :].astype(F32)
@@ -367,54 +358,59 @@
         return sent_ref[rows, :].astype(F32) + got_ref[rows, :].astype(F32)
 
 
-def step_kernel(sent_ref, got_ref, keep_ref, message_ref, next_keep_ref, *, now, then):
+def step_kernel(sent_ref, got_ref, keep_ref, message_ref, next_keep_ref, *tail_refs, now, then):
     message_ref[0 : now.weights, :] = now.weight_sum(sent_ref, got_ref).astype(BF16)
     other = now.tail(got_ref)
     halo, hubs = now.merged(keep_ref[...], other)
-    then.write(message_ref, next_keep_ref, halo, hubs, now.bias(now.tail(sent_ref), other))
-
-
-def returned_kernel(got_ref, keep_ref, rows_ref, *, now):
-    halo, hubs = now.merged(keep_ref[...], now.tail(got_ref))
-    rows_ref[...] = jnp.concatenate([halo, hubs], axis=0)
-
-
-def weights_kernel(sent_ref, got_ref, w_self_ref, w_neigh_ref, bias_ref, *, now):
-    total = now.weight_sum(sent_ref, got_ref)
-    split = now.weights // 2
-    w_self_ref[...] = jnp.transpose(total[:split])
-    w_neigh_ref[...] = jnp.transpose(total[split:])
-    bias_ref[...] = now.bias(now.tail(sent_ref), now.tail(got_ref))
-
-
-def features_kernel(
-    rows_ref, count_ref, owner_ref, hub_row_ref, partial_ref, other_partial_ref, own_rows_ref, other_rows_ref,
-    low_ref, total_ref, returned_ref,
+    sent = then.write(message_ref, next_keep_ref, halo, hubs, now.bias(now.tail(sent_ref), other))
+    for tail_ref in tail_refs:
+        tail_ref[...] = sent
+
+
+def prepare_kernel(
+    rows_ref, count_ref, owner_ref, hub_row_ref, partial_ref, other_partial_ref, total_ref, target_ref
 ):
     me = lax.axis_index("dom")
     slots, partitions = rows_ref.shape
+    nodes = partial_ref.shape[0]
     steps = partitions.bit_length() - 1
     total_ref[...] = partial_ref[...] + other_partial_ref[...]
-    returned_ref[...] = own_rows_ref[...] + other_rows_ref[...]
-
     for group in range(partitions):
         origin = me ^ sum(((group >> k) & 1) << (steps - 1 - k) for k in range(steps))
         for slot in range(slots):
-            row = pl.ds(rows_ref[slot, origin], 1)
-            place = group * slots + slot
-            total_ref[row, :] += jnp.where(slot < count_ref[origin], returned_ref[place : place + 1, :], 0.0)
+            sent = slot < count_ref[origin]
+            target_ref[group * slots + slot] = jnp.where(sent, rows_ref[slot, origin], nodes)
+    base = partitions * slots
+    for slot in range(HUB_MOST):
+        target_ref[base + slot] = nodes
 
     def hub(index, slot):
-        mine = owner_ref[index] == me
-
-        @pl.when(mine)
-        def _():
-            total_ref[pl.ds(hub_row_ref[index], 1), :] += returned_ref[pl.ds(partitions * slots + slot, 1), :]
-
-        return slot + mine.astype(jnp.int32)
+        mine = (owner_ref[index] == me).astype(jnp.int32)
+        target_ref[base + slot] = jnp.where(mine == 1, hub_row_ref[index], nodes)
+        return slot + mine
 
     repeat(owner_ref.shape[0], hub, jnp.int32(0))
-    low_ref[...] = total_ref[...].astype(BF16)
+
+
+def final_kernel(
+    target_ref, sent_ref, got_ref, cross_ref, keep_ref, other_keep_ref, total_in_ref,
+    w_self_ref, w_neigh_ref, bias_ref, low_ref, total_ref, *, now,
+):
+    nodes = total_in_ref.shape[0]
+    total_ref[0:nodes, :] = total_in_ref[...]
+    got = now.tail(got_ref)
+    keep = keep_ref[...] + other_keep_ref[...]
+    halo, hubs = now.merged(keep, got + cross_ref[...].astype(F32))
+    returned = jnp.concatenate([halo, hubs], axis=0)
+    for place in range(returned.shape[0]):
+        row = pl.ds(target_ref[place], 1)
+        total_ref[row, :] += returned[place : place + 1, :]
+    low_ref[...] = total_ref[0:nodes, :].astype(BF16)
+    weights = now.weight_sum(sent_ref, got_ref)
+    split = now.weights // 2
+    w_self_ref[...] = jnp.transpose(weights[:split])
+    w_neigh_ref[...] = jnp.transpose(weights[split:])
+    bias_ref[...] = now.bias(now.tail(sent_ref), got)
 
 
 SMEM = pl.BlockSpec(memory_space=pltpu.SMEM)
@@ -452,7 +448,7 @@
     counts = send_count.reshape(partitions)
     owner = hub_owner.reshape(hubs)
     struct = jax.ShapeDtypeStruct
-    lists = pltpu.SMEM((3, limit + GROUP_TILES), jnp.int32)
+    lists = pltpu.SMEM((limit + GROUP_TILES,), jnp.int32)
 
     bundle = call(
         gather_kernel, "gather", [HBM] * 5,
@@ -487,7 +483,7 @@
             pltpu.VMEM(adjacency.shape, BF16),
             pltpu.VMEM((dst_blocks + 1, tile_rows, hidden), BF16),
             pltpu.VMEM((dst_blocks + 1, tile_rows, hidden), F32),
-            pltpu.VMEM((dst_blocks, far_blocks, tile_rows, columns), F32),
+            pltpu.VMEM((dst_blocks + 1, far_blocks, tile_rows, columns), F32),
             pltpu.VMEM((dst_blocks, tile_rows, far_blocks * columns), BF16),
             lists,
             lists,
@@ -516,7 +512,6 @@
             pltpu.VMEM((dst_blocks, tile_rows, far_blocks * columns), BF16),
             pltpu.VMEM((far_blocks * columns, inputs), F32),
             pltpu.VMEM((far_blocks * columns, inputs), BF16),
-            pltpu.VMEM((dst_blocks, tile_rows, hidden), BF16),
             pltpu.VMEM((dst_blocks + 1, hidden, tile_rows), BF16),
             pltpu.VMEM((dst_blocks + 1, hidden, tile_rows), F32),
             pltpu.VMEM((far_blocks * columns, inputs), F32),
@@ -532,31 +527,38 @@
         ),
         50, out_specs=(HBM, VMEM, VMEM, VMEM),
     )
-    other_partial = lax.ppermute(partial, "feat", [(0, 1), (1, 0)])
-    for now in plans:
+    swap = [(0, 1), (1, 0)]
+    tail = None
+    for now, then in zip(plans, plans[1:]):
         got = lax.ppermute(message, "dom", [(q, q ^ now.half) for q in range(partitions)])
-        if now is plans[-1]:
-            break
-        then = plans[plans.index(now) + 1]
-        message, keep = call(
+        if now is plans[0]:
+            got, late_partial = lax.optimization_barrier((got, partial))
+        outs = [struct((then.rows, inputs), BF16), struct((then.keep, inputs), F32)]
+        if then is plans[-1]:
+            outs.append(struct((then.rows - then.weights, inputs), BF16))
+        message, keep, *tail = call(
             functools.partial(step_kernel, now=now, then=then), "step", [VMEM] * 3,
-            (struct((then.rows, inputs), BF16), struct((then.keep, inputs), F32)),
-            [], (message, got, keep), 16,
+            tuple(outs), [], (message, got, keep), 16,
         )
-    own_rows = call(
-        functools.partial(returned_kernel, now=now), "returned", [VMEM] * 2,
-        struct((2 * now.halo + now.hub, inputs), F32), [], (got, keep), 16,
-    )
-    other_rows = lax.ppermute(own_rows, "feat", [(0, 1), (1, 0)])
-    grad_w_self, grad_w_neigh, grad_bias = call(
-        functools.partial(weights_kernel, now=now), "weights", [VMEM] * 2,
-        (struct((inputs, hidden), F32), struct((inputs, hidden), F32), struct((1, hidden), F32)),
-        [], (message, got), 16,
-    )
-    grad_features = call(
-        features_kernel, "features", [SMEM] * 4 + [VMEM] * 4, struct((nodes, inputs), BF16),
-        [pltpu.VMEM((nodes, inputs), F32), pltpu.VMEM((2 * now.halo + now.hub, inputs), F32)],
-        (rows, counts, owner, hub_row, partial, other_partial, own_rows, other_rows), 32,
+    now = plans[-1]
+    got = lax.ppermute(message, "dom", [(q, q ^ 1) for q in range(partitions)])
+    cross = lax.ppermute(tail[0], ("dom", "feat"), [(k, k ^ 3) for k in range(2 * partitions)])
+    other_keep = lax.ppermute(keep, "feat", swap)
+    other_partial = lax.ppermute(late_partial, "feat", swap)
+    summed, target = call(
+        prepare_kernel, "prepare", [SMEM] * 4 + [VMEM] * 2,
+        (struct((nodes, inputs), F32), struct((partitions * slots + HUB_MOST,), jnp.int32)),
+        [], (rows, counts, owner, hub_row, partial, other_partial), 16,
+        flops=10**6, size=4 * 10**6, out_specs=(VMEM, SMEM),
+    )
+    grad_w_self, grad_w_neigh, grad_bias, grad_features = call(
+        functools.partial(final_kernel, now=now), "final", [SMEM] + [VMEM] * 6,
+        (
+            struct((inputs, hidden), F32), struct((inputs, hidden), F32), struct((1, hidden), F32),
+            struct((nodes, inputs), BF16),
+        ),
+        [pltpu.VMEM((nodes + 8, inputs), F32)],
+        (target, message, got, cross, keep, other_keep, summed), 32,
     )
     return (output, grad_features, grad_w_self, grad_w_neigh, grad_bias.reshape(hidden))
 

time: 40.9 us -> 39.2 us (0.958)
  waiting for transfers between devices: 14.3 us -> 12.8 us
    ppermute x3 -> x2, starting transfers between devices: 5.49 us -> 1.72 us  [local(): lax.ppermute(message, 'dom', [(q, q ^ now.half) for q in range(partitions)])]
    ppermute x2 -> x4, starting transfers between devices: 0.07 us -> 3.51 us  [the longest x1 3.3 us: local(): got = lax.ppermute(message, 'dom', [(q, q ^ 1) for q in range(partitions)])]
    ppermute x3 -> x2, waiting for transfers between devices: 11.5 us -> 8.94 us  [local(): lax.ppermute(message, 'dom', [(q, q ^ now.half) for q in range(partitions)])]
    ppermute x2 -> x4, waiting for transfers between devices: 0.42 us -> 1.56 us  [the longest x1 1.55 us: local(): lax.ppermute(tail[0], ('dom', 'feat'), [(k, k ^ 3) for k in range(2 * par...]
    pallas_call x8 -> x7, Pallas kernels: 12.1 us -> 12.5 us  [call(): pl.pallas_call(kernel, out_shape=outs, in_specs=ins, out_specs=jax.tree.m...]
  transfers between devices with their start and end apart: 6 -> 7, of which waited for: 5 -> 4; matrix products, arithmetic and copies ran while one was open for 0% -> 0% of each run, Pallas kernels for 11% -> 13%
where the time goes in v4:
time: 39.2 us; the launch traced here: 39.3 us
  waiting for transfers between devices  12.8 us (33%)
  Pallas kernels  12.5 us (32%)
  starting transfers between devices  12.5 us (32%)
  between operations  1.46 us (4%)
    pallas_call x7, Pallas kernels, call(): pl.pallas_call(kernel, out_shape=outs, in_specs=ins, out_specs=jax.tree.m...  12.5 us
    ppermute x2, waiting for transfers between devices, local(): lax.ppermute(message, 'dom', [(q, q ^ now.half) for q in range(partitions)])  8.94 us
    all_to_all x1, starting transfers between devices, local(): lax.all_to_all(bundle, 'dom', split_axis=0, concat_axis=0, tiled=True)  7.26 us
    ppermute x1, starting transfers between devices, local(): got = lax.ppermute(message, 'dom', [(q, q ^ 1) for q in range(partitions)])  3.3 us
    all_to_all x1, waiting for transfers between devices, local(): lax.all_to_all(bundle, 'dom', split_axis=0, concat_axis=0, tiled=True)  2.31 us
    ppermute x2, starting transfers between devices, local(): lax.ppermute(message, 'dom', [(q, q ^ now.half) for q in range(partitions)])  1.72 us
    ppermute x1, waiting for transfers between devices, local(): lax.ppermute(tail[0], ('dom', 'feat'), [(k, k ^ 3) for k in range(2 * par...  1.55 us
  transfers between devices with their start and end apart: 7, of which 4 were waited for; matrix products, arithmetic and copies ran while one was open for 0% of the time, Pallas kernels for 13%

profile of v4, /device:TPU:0, one launch (start us, length us, event | category | flops | bytes accessed | tf_op | source)
XLA Modules:
  0.0 39.3 jit_solution(9595584353408377467)
XLA Ops:
  0.6 0.0 copy-start
  0.6 0.0 copy-start.4
  0.7 0.0 copy-start.7
  0.7 0.0 copy-start.6
  0.7 0.0 copy-start.3
  0.7 0.0 copy-start.2
  0.7 0.0 copy-start.1
  0.7 1.8 %gather.1 = f32[8,8,128]{2,1,0:T(8,128)} custom-call(s32[2,8]{1,0:T(2,128)} %bitcast.10, s32[8]{0:T(128)} %bitcast.12, s32[16]{0:T(128)} %bitcast.7, s32[16]{0:T(128)} %hub_row_ref.1, bf16[1024,128]{1,0:T(8,128)(2,1)} %features_ref.1), custom_call_target="tpu_custom_call" | custom-call | tf_op jit(solution)/shard_map/gather/pallas_call | solution.py:422
  2.5 7.3 %all-to-all-start = ((f32[8,8,128]{2,1,0:T(8,128)}), f32[8,8,128]{2,1,0:T(8,128)S(1)}, u32[]{:S(2)}, u32[]{:S(2)}) async-start(f32[8,8,128]{2,1,0:T(8,128)} %gather.1), calls=%async_computation | async-start | bytes 65536 | tf_op jit(solution)/shard_map/all_to_all | solution.py:468
  10.5 3.7 %own_tiles.1 = (f32[56,256,128]{2,1,0:T(8,128)}, bf16[56,256,256]{2,1,0:T(8,128)(2,1)}) custom-call(s32[56]{0:T(128)} %dst_ref.1, s32[56]{0:T(128)} %src_ref.1, s32[1]{0:T(128)S(6)} %copy.18.count_hbm.count_ref, bf16[1024,128]{1,0:T(8,128)(2,1)} %features_ref.1, bf16[128,128]{1,0:T(8,128)(2,1)} %w_self_ref.1, bf16[128,128]{1,0:T(8,128)(2,1)} %w_neigh_ref.1, ...), custom_call_target="tpu_custom_call" | custom-call | flops 939524096 | bytes 7340032 | tf_op jit(solution)/shard_map/own_tiles/pallas_call | solution.py:422
  14.2 2.3 %all-to-all-done.arrived_ref = f32[8,8,128]{2,1,0:T(8,128)S(1)} async-done(((f32[8,8,128]{2,1,0:T(8,128)}), f32[8,8,128]{2,1,0:T(8,128)S(1)}, u32[]{:S(2)}, u32[]{:S(2)}) %all-to-all-start) | async-done | bytes 32800 | tf_op jit(solution)/shard_map/all_to_all | solution.py:468
  16.5 0.0 copy-done
  16.5 0.0 copy-done.4
  16.5 0.0 copy-done.7
  16.5 0.0 copy-done.6
  16.5 0.0 copy-done.3
  16.5 0.0 copy-done.2
  16.5 0.0 copy-done.1
  16.5 0.0 copy-start.5
  16.5 0.0 copy-start.8
  16.6 0.0 copy-start.9
  16.6 4.2 %rest.1 = (bf16[1024,128]{1,0:T(8,128)(2,1)}, f32[1024,128]{1,0:T(8,128)S(1)}, bf16[288,128]{1,0:T(8,128)(2,1)S(1)}, f32[24,128]{1,0:T(8,128)S(1)}) custom-call(s32[56]{0:T(128)S(1)} %copy-done.6, s32[56]{0:T(128)S(1)} %copy-done.7, s32[1]{0:T(128)S(6)} %copy.18.count_hbm.count_ref, s32[16]{0:T(128)S(1)} %bitcast.8, ...), custom_call_target="tpu_custom_call" | custom-call | tf_op jit(solution)/shard_map/rest/pallas_call | solution.py:422
  20.8 1.7 %collective-permute-start = (bf16[288,128]{1,0:T(8,128)(2,1)S(1)}, bf16[288,128]{1,0:T(8,128)(2,1)S(1)}, u32[]{:S(2)}, u32[]{:S(2)}) collective-permute-start(bf16[288,128]{1,0:T(8,128)(2,1)S(1)} %get-tuple-element.28.sent_ref), channel_id=1, source_target_pairs={{0,8},{2,10},{4,12},{6,14},{8,0},{10,2},{12,4},{14,6},{1,9},{3,11}... | collective-permute-start | bytes 221192 | tf_op jit(solution)/shard_map/ppermute | solution.py:533
  22.4 4.3 %collective-permute-done.got_ref = bf16[288,128]{1,0:T(8,128)(2,1)S(1)} collective-permute-done((bf16[288,128]{1,0:T(8,128)(2,1)S(1)}, bf16[288,128]{1,0:T(8,128)(2,1)S(1)}, u32[]{:S(2)}, u32[]{:S(2)}) %collective-permute-start) | collective-permute-done | bytes 73760 | tf_op jit(solution)/shard_map/ppermute | solution.py:533
  26.7 0.0 collective-permute-start.1
  26.8 0.1 collective-permute-start.2
  26.8 4.7 %collective-permute-done.2.got_ref = bf16[288,128]{1,0:T(8,128)(2,1)S(1)} collective-permute-done((bf16[288,128]{1,0:T(8,128)(2,1)S(1)}, bf16[288,128]{1,0:T(8,128)(2,1)S(1)}, u32[]{:S(2)}, u32[]{:S(2)}) %collective-permute-start.2) | collective-permute-done | bytes 73760 | tf_op jit(solution)/shard_map/ppermute | solution.py:533
  31.5 3.3 %collective-permute-start.3 = (bf16[272,128]{1,0:T(8,128)(2,1)S(1)}, bf16[272,128]{1,0:T(8,128)(2,1)S(1)}, u32[]{:S(2)}, u32[]{:S(2)}) collective-permute-start(bf16[272,128]{1,0:T(8,128)(2,1)S(1)} %get-tuple-element.35.sent_ref), channel_id=1, source_target_pairs={{0,2},{2,0},{4,6},{6,4},{8,10},{10,8},{12,14},{14,12},{1,3},{3,1},... | collective-permute-start | bytes 208904 | tf_op jit(solution)/shard_map/ppermute | solution.py:544
  34.8 0.0 collective-permute-start.5
  34.8 0.2 collective-permute-start.4
  35.0 0.0 collective-permute-done.1.other_partial_ref
  35.0 0.0 copy-done.5
  35.0 0.0 copy-done.8
  35.1 0.0 copy-done.9
  35.1 1.2 %prepare.1 = (f32[1024,128]{1,0:T(8,128)S(1)}, s32[20]{0:T(128)S(1)}) custom-call(s32[2,8]{1,0:T(2,128)S(1)} %bitcast.11, s32[8]{0:T(128)S(1)} %bitcast.13, s32[16]{0:T(128)S(1)} %bitcast.9, s32[16]{0:T(128)S(1)} %copy-done.9, f32[1024,128]{1,0:T(8,128)S(1)} %get-tuple-element.29.partial_ref, f32[1024,128]{1,0:T(8,128)S(1)} %collective-permute-done.1.other_partial_ref), custom_call_target="tpu_custom_call" | custom-call | flops 1000000 | bytes 4000000 | tf_op jit(solution)/shard_map/prepare/pallas_call | solution.py:422
  36.3 1.5 %collective-permute-done.4.cross_ref = bf16[16,128]{1,0:T(8,128)(2,1)S(1)} collective-permute-done((bf16[16,128]{1,0:T(8,128)(2,1)S(1)}, bf16[16,128]{1,0:T(8,128)(2,1)S(1)}, u32[]{:S(2)}, u32[]{:S(2)}) %collective-permute-start.4) | collective-permute-done | bytes 4128 | tf_op jit(solution)/shard_map/ppermute | solution.py:545
  37.9 0.0 collective-permute-done.5.other_keep_ref
  37.9 0.0 collective-permute-done.3.got_ref
  37.9 1.4 %final.1 = (f32[128,128]{1,0:T(8,128)}, f32[128,128]{1,0:T(8,128)}, f32[1,128]{1,0:T(1,128)}, bf16[1024,128]{1,0:T(8,128)(2,1)}) custom-call(s32[20]{0:T(128)S(1)} %get-tuple-element.30.target_ref, bf16[272,128]{1,0:T(8,128)(2,1)S(1)} %get-tuple-element.35.sent_ref, bf16[272,128]{1,0:T(8,128)(2,1)S(1)} %collective-permute-done.3.got_ref, ...), custom_call_target="tpu_custom_call" | custom-call | tf_op jit(solution)/shard_map/final/pallas_call | solution.py:422
  (2 shorter events, 0.1 us)
Async XLA Ops:
  0.6 15.9 %copy-start = (bf16[1024,128]{1,0:T(8,128)(2,1)S(1)}, bf16[1024,128]{1,0:T(8,128)(2,1)}, u32[]{:S(2)}) copy-start(bf16[1024,128]{1,0:T(8,128)(2,1)} %features_ref.1) | copy-start | bytes 786436
  0.6 15.8 %copy-start.4 = (s32[16,1]{0,1:T(1,128)S(1)}, s32[16,1]{0,1:T(1,128)}, u32[]{:S(2)}) copy-start(s32[16,1]{0,1:T(1,128)} %param.24) | copy-start | bytes 196
  0.7 15.8 %copy-start.7 = (s32[56]{0:T(128)S(1)}, s32[56]{0:T(128)}, u32[]{:S(2)}) copy-start(s32[56]{0:T(128)} %src_ref.1) | copy-start | bytes 676
  0.7 15.8 %copy-start.6 = (s32[56]{0:T(128)S(1)}, s32[56]{0:T(128)}, u32[]{:S(2)}) copy-start(s32[56]{0:T(128)} %dst_ref.1) | copy-start | bytes 676
  0.7 15.8 %copy-start.3 = (bf16[128,128]{1,0:T(8,128)(2,1)S(1)}, bf16[128,128]{1,0:T(8,128)(2,1)}, u32[]{:S(2)}) copy-start(bf16[128,128]{1,0:T(8,128)(2,1)} %w_neigh_ref.1) | copy-start | bytes 98308
  0.7 15.8 %copy-start.2 = (bf16[128,128]{1,0:T(8,128)(2,1)S(1)}, bf16[128,128]{1,0:T(8,128)(2,1)}, u32[]{:S(2)}) copy-start(bf16[128,128]{1,0:T(8,128)(2,1)} %w_self_ref.1) | copy-start | bytes 98308
  0.7 15.8 %copy-start.1 = (bf16[1024,128]{1,0:T(8,128)(2,1)S(1)}, bf16[1024,128]{1,0:T(8,128)(2,1)}, u32[]{:S(2)}) copy-start(bf16[1024,128]{1,0:T(8,128)(2,1)} %cotangent_ref.1) | copy-start | bytes 786436
  2.5 14.0 %all-to-all-start = ((f32[8,8,128]{2,1,0:T(8,128)}), f32[8,8,128]{2,1,0:T(8,128)S(1)}, u32[]{:S(2)}, u32[]{:S(2)}) async-start(f32[8,8,128]{2,1,0:T(8,128)} %gather.1), calls=%async_computation | async-start | bytes 65536 | tf_op jit(solution)/shard_map/all_to_all | solution.py:468
  16.5 18.5 %copy-start.5 = (s32[1,8,2]{1,2,0:T(2,128)S(1)}, s32[1,8,2]{1,2,0:T(2,128)}, u32[]{:S(2)}) copy-start(s32[1,8,2]{1,2,0:T(2,128)} %param.22) | copy-start | bytes 196
  16.5 18.5 %copy-start.8 = (s32[1,8]{1,0:T(1,128)S(1)}, s32[1,8]{1,0:T(1,128)}, u32[]{:S(2)}) copy-start(s32[1,8]{1,0:T(1,128)} %param.23) | copy-start | bytes 100
  16.6 18.5 %copy-start.9 = (s32[16]{0:T(128)S(1)}, s32[16]{0:T(128)}, u32[]{:S(2)}) copy-start(s32[16]{0:T(128)} %hub_row_ref.1) | copy-start | bytes 196
  20.8 5.9 %collective-permute-start = (bf16[288,128]{1,0:T(8,128)(2,1)S(1)}, bf16[288,128]{1,0:T(8,128)(2,1)S(1)}, u32[]{:S(2)}, u32[]{:S(2)}) collective-permute-start(bf16[288,128]{1,0:T(8,128)(2,1)S(1)} %get-tuple-element.28.sent_ref), channel_id=1, source_target_pairs={{0,8},{2,10},{4,12},{6,14},{8,0},{10,2},{12,4},{14,6},{1,9},{3,11}... | collective-permute-start | bytes 221192 | tf_op jit(solution)/shard_map/ppermute | solution.py:533
  26.7 8.3 %collective-permute-start.1 = (f32[1024,128]{1,0:T(8,128)S(1)}, f32[1024,128]{1,0:T(8,128)S(1)}, u32[]{:S(2)}, u32[]{:S(2)}) collective-permute-start(f32[1024,128]{1,0:T(8,128)S(1)} %get-tuple-element.29.partial_ref), channel_id=1, source_target_pairs={{0,1},{1,0},{2,3},{3,2},{4,5},{5,4},{6,7},{7,6},{8,9},{9,8},{10,11... | collective-permute-start | bytes 1572872 | tf_op jit(solution)/shard_map/ppermute | solution.py:547
  26.8 4.7 %collective-permute-start.2 = (bf16[288,128]{1,0:T(8,128)(2,1)S(1)}, bf16[288,128]{1,0:T(8,128)(2,1)S(1)}, u32[]{:S(2)}, u32[]{:S(2)}) collective-permute-start(bf16[288,128]{1,0:T(8,128)(2,1)S(1)} %get-tuple-element.33.sent_ref), channel_id=1, source_target_pairs={{0,4},{2,6},{4,0},{6,2},{8,12},{10,14},{12,8},{14,10},{1,5},{3,7},... | collective-permute-start | bytes 221192 | tf_op jit(solution)/shard_map/ppermute | solution.py:533
  31.5 6.3 %collective-permute-start.3 = (bf16[272,128]{1,0:T(8,128)(2,1)S(1)}, bf16[272,128]{1,0:T(8,128)(2,1)S(1)}, u32[]{:S(2)}, u32[]{:S(2)}) collective-permute-start(bf16[272,128]{1,0:T(8,128)(2,1)S(1)} %get-tuple-element.35.sent_ref), channel_id=1, source_target_pairs={{0,2},{2,0},{4,6},{6,4},{8,10},{10,8},{12,14},{14,12},{1,3},{3,1},... | collective-permute-start | bytes 208904 | tf_op jit(solution)/shard_map/ppermute | solution.py:544
  34.8 3.0 %collective-permute-start.5 = (f32[12,128]{1,0:T(8,128)S(1)}, f32[12,128]{1,0:T(8,128)S(1)}, u32[]{:S(2)}, u32[]{:S(2)}) collective-permute-start(f32[12,128]{1,0:T(8,128)S(1)} %get-tuple-element.37.keep_ref), channel_id=1, source_target_pairs={{0,1},{1,0},{2,3},{3,2},{4,5},{5,4},{6,7},{7,6},{8,9},{9,8},{10,11... | collective-permute-start | bytes 18440 | tf_op jit(solution)/shard_map/ppermute | solution.py:546
  34.8 3.0 %collective-permute-start.4 = (bf16[16,128]{1,0:T(8,128)(2,1)S(1)}, bf16[16,128]{1,0:T(8,128)(2,1)S(1)}, u32[]{:S(2)}, u32[]{:S(2)}) collective-permute-start(bf16[16,128]{1,0:T(8,128)(2,1)S(1)} %get-tuple-element.36), channel_id=1, source_target_pairs={{0,3},{1,2},{2,1},{3,0},{4,7},{5,6},{6,5},{7,4},{8,11},{9,10},{10,... | collective-permute-start | bytes 12296 | tf_op jit(solution)/shard_map/ppermute | solution.py:545

commit v5 on v4

--- a/solution.py
+++ b/solution.py
@@ -203,11 +203,11 @@
 
 
 def rest_kernel(
-    dst_ref, src_ref, count_ref, owner_ref,
+    dst_hbm, src_hbm, count_hbm, owner_hbm,
     arrived_ref, total_hbm, far_hbm, features_ref, w_self_ref, w_neigh_ref, cotangent_ref, adjacency_hbm,
     output_hbm, partial_ref, message_ref, keep_ref,
     halo_ref, hubs_ref, output_ref, total_ref, far_ref, rows_ref, low_rows_ref, grad_t_ref, source_t_ref,
-    back_ref, adjacency_ref, list_ref, counter_ref, tile_sems, sems,
+    back_ref, adjacency_ref, list_ref, counter_ref, dst_ref, src_ref, count_ref, owner_ref, tile_sems, sems, scalar_sems,
     *, partitions, slots, columns,
 ):
     me = lax.axis_index("dom")
@@ -215,11 +215,18 @@
     dst_blocks = total_ref.shape[0]
     halo_blocks = -(-partitions * slots // tile_rows)
     hub_base = halo_blocks * columns
+    scalars = fetch(
+        [(src_hbm, src_ref), (dst_hbm, dst_ref), (count_hbm, count_ref), (owner_hbm, owner_ref)], scalar_sems
+    )
     total_in = pltpu.make_async_copy(total_hbm.at[0:dst_blocks], total_ref, sems.at[0])
     total_in.start()
     far_in = pltpu.make_async_copy(far_hbm.at[0:dst_blocks], far_ref, sems.at[1])
     far_in.start()
-
+    rows_ref[...] = jnp.zeros_like(rows_ref)
+    source_t_ref[...] = jnp.zeros_like(source_t_ref)
+    grad_t_ref[dst_blocks] = jnp.zeros(grad_t_ref.shape[1:], BF16)
+    for copy in scalars:
+        copy.wait()
     near = Tiles(list_ref, adjacency_hbm, adjacency_ref, tile_sems)
 
     def find_near(tile, used):
@@ -235,8 +242,6 @@
 
     used = lax.fori_loop(0, count_ref[0], find_near, jnp.int32(0))
     pad_list(list_ref, used, dst_blocks, dst_blocks, GROUP_TILES)
-
-    rows_ref[...] = jnp.zeros_like(rows_ref)
 
     def halo_in(q, carry):
         rows_ref[pl.ds(q * slots, slots), :] = arrived_ref[q, 0:slots, :]
@@ -275,8 +280,6 @@
         far_t += dot(low_t, far_ref[block])
     output_out = pltpu.make_async_copy(output_ref, output_hbm, sems.at[2])
     output_out.start()
-    grad_t_ref[dst_blocks] = jnp.zeros(grad_t_ref.shape[1:], BF16)
-    source_t_ref[...] = jnp.zeros_like(source_t_ref)
 
     def backward(tile, dst, src):
         source_t_ref[src] += dot(grad_t_ref[dst], adjacency_ref[tile])
@@ -393,15 +396,18 @@
 
 
 def final_kernel(
-    target_ref, sent_ref, got_ref, cross_ref, keep_ref, other_keep_ref, total_in_ref,
-    w_self_ref, w_neigh_ref, bias_ref, low_ref, total_ref, *, now,
+    target_hbm, sent_ref, got_ref, cross_ref, keep_ref, other_keep_ref, total_in_ref,
+    w_self_ref, w_neigh_ref, bias_ref, low_ref, total_ref, target_ref, sem, *, now,
 ):
     nodes = total_in_ref.shape[0]
+    target_in = pltpu.make_async_copy(target_hbm, target_ref, sem)
+    target_in.start()
     total_ref[0:nodes, :] = total_in_ref[...]
     got = now.tail(got_ref)
     keep = keep_ref[...] + other_keep_ref[...]
     halo, hubs = now.merged(keep, got + cross_ref[...].astype(F32))
     returned = jnp.concatenate([halo, hubs], axis=0)
+    target_in.wait()
     for place in range(returned.shape[0]):
         row = pl.ds(target_ref[place], 1)
         total_ref[row, :] += returned[place : place + 1, :]
@@ -497,7 +503,7 @@
     plans = [Exchange(partitions, slots, step) for step in range(partitions.bit_length() - 1)]
     output, partial, message, keep = call(
         functools.partial(rest_kernel, partitions=partitions, slots=slots, columns=columns), "rest",
-        [SMEM] * 4 + [VMEM, HBM, HBM] + [VMEM] * 4 + [HBM],
+        [HBM] * 4 + [VMEM, HBM, HBM] + [VMEM] * 4 + [HBM],
         (
             struct((nodes, hidden), BF16),
             struct((nodes, inputs), F32),
@@ -518,8 +524,13 @@
             pltpu.VMEM(adjacency.shape, BF16),
             lists,
             pltpu.SMEM((partitions,), jnp.int32),
+            pltpu.SMEM((limit,), jnp.int32),
+            pltpu.SMEM((limit,), jnp.int32),
+            pltpu.SMEM((1,), jnp.int32),
+            pltpu.SMEM((hubs,), jnp.int32),
             pltpu.SemaphoreType.DMA((limit,)),
             pltpu.SemaphoreType.DMA((3,)),
+            pltpu.SemaphoreType.DMA((4,)),
         ],
         (
             tile_dst, tile_src, tile_count, owner,
@@ -552,12 +563,16 @@
         flops=10**6, size=4 * 10**6, out_specs=(VMEM, SMEM),
     )
     grad_w_self, grad_w_neigh, grad_bias, grad_features = call(
-        functools.partial(final_kernel, now=now), "final", [SMEM] + [VMEM] * 6,
+        functools.partial(final_kernel, now=now), "final", [HBM] + [VMEM] * 6,
         (
             struct((inputs, hidden), F32), struct((inputs, hidden), F32), struct((1, hidden), F32),
             struct((nodes, inputs), BF16),
         ),
-        [pltpu.VMEM((nodes + 8, inputs), F32)],
+        [
+            pltpu.VMEM((nodes + 8, inputs), F32),
+            pltpu.SMEM((partitions * slots + HUB_MOST,), jnp.int32),
+            pltpu.SemaphoreType.DMA,
+        ],
         (target, message, got, cross, keep, other_keep, summed), 32,
     )
     return (output, grad_features, grad_w_self, grad_w_neigh, grad_bias.reshape(hidden))

time: 39.2 us -> 39 us (level); the launches traced: 39.3 us -> 38.5 us
  waiting for transfers between devices: 12.8 us -> 9.51 us
  starting transfers between devices: 12.5 us -> 15.4 us
  Pallas kernels: 12.5 us -> 12.1 us
    ppermute x2, starting transfers between devices: 1.72 us -> 5.91 us  [local(): lax.ppermute(message, 'dom', [(q, q ^ now.half) for q in range(partitions)])]
    ppermute x1, starting transfers between devices: 3.3 us -> 0.07 us  [local(): got = lax.ppermute(message, 'dom', [(q, q ^ 1) for q in range(partitions)])]
    ppermute x2, waiting for transfers between devices: 8.94 us -> 6.48 us  [local(): lax.ppermute(message, 'dom', [(q, q ^ now.half) for q in range(partitions)])]
    ppermute x1, starting transfers between devices: 0.2 us -> 2.05 us  [local(): lax.ppermute(tail[0], ('dom', 'feat'), [(k, k ^ 3) for k in range(2 * par...]
    ppermute x1, waiting for transfers between devices: 1.55 us -> 0.05 us  [local(): lax.ppermute(tail[0], ('dom', 'feat'), [(k, k ^ 3) for k in range(2 * par...]
    ppermute x1, waiting for transfers between devices: 0.01 us -> 0.84 us  [local(): got = lax.ppermute(message, 'dom', [(q, q ^ 1) for q in range(partitions)])]
where the time goes in v5:
time: 39 us; the launch traced here: 38.5 us
  starting transfers between devices  15.4 us (39%)
  Pallas kernels  12.1 us (31%)
  waiting for transfers between devices  9.51 us (24%)
  between operations  1.46 us (4%)
    pallas_call x7, Pallas kernels, call(): pl.pallas_call(kernel, out_shape=outs, in_specs=ins, out_specs=jax.tree.m...  12.1 us
    all_to_all x1, starting transfers between devices, local(): lax.all_to_all(bundle, 'dom', split_axis=0, concat_axis=0, tiled=True)  7.26 us
    ppermute x2, waiting for transfers between devices, local(): lax.ppermute(message, 'dom', [(q, q ^ now.half) for q in range(partitions)])  6.48 us
    ppermute x2, starting transfers between devices, local(): lax.ppermute(message, 'dom', [(q, q ^ now.half) for q in range(partitions)])  5.91 us
    all_to_all x1, waiting for transfers between devices, local(): lax.all_to_all(bundle, 'dom', split_axis=0, concat_axis=0, tiled=True)  2.13 us
    ppermute x1, starting transfers between devices, local(): lax.ppermute(tail[0], ('dom', 'feat'), [(k, k ^ 3) for k in range(2 * par...  2.05 us
    ppermute x1, waiting for transfers between devices, local(): got = lax.ppermute(message, 'dom', [(q, q ^ 1) for q in range(partitions)])  0.84 us
  transfers between devices with their start and end apart: 7, of which 4 were waited for; matrix products, arithmetic and copies ran while one was open for 0% of the time, Pallas kernels for 13%

profile of v5, /device:TPU:0, one launch (start us, length us, event | category | flops | bytes accessed | tf_op | source)
XLA Modules:
  0.0 38.5 jit_solution(572270262437349916)
XLA Ops:
  0.6 0.0 copy-start
  0.6 0.0 copy-start.4
  0.7 0.0 copy-start.7
  0.7 0.0 copy-start.6
  0.7 0.0 copy-start.3
  0.7 0.0 copy-start.2
  0.7 0.0 copy-start.1
  0.7 1.8 %gather.1 = f32[8,8,128]{2,1,0:T(8,128)} custom-call(s32[2,8]{1,0:T(2,128)} %bitcast.10, s32[8]{0:T(128)} %bitcast.12, s32[16]{0:T(128)} %bitcast.7, s32[16]{0:T(128)} %hub_row_ref.1, bf16[1024,128]{1,0:T(8,128)(2,1)} %features_ref.1), custom_call_target="tpu_custom_call" | custom-call | tf_op jit(solution)/shard_map/gather/pallas_call | solution.py:428
  2.5 7.3 %all-to-all-start = ((f32[8,8,128]{2,1,0:T(8,128)}), f32[8,8,128]{2,1,0:T(8,128)S(1)}, u32[]{:S(2)}, u32[]{:S(2)}) async-start(f32[8,8,128]{2,1,0:T(8,128)} %gather.1), calls=%async_computation | async-start | bytes 65536 | tf_op jit(solution)/shard_map/all_to_all | solution.py:474
  10.4 3.9 %own_tiles.1 = (f32[56,256,128]{2,1,0:T(8,128)}, bf16[56,256,256]{2,1,0:T(8,128)(2,1)}) custom-call(s32[56]{0:T(128)} %dst_hbm.3, s32[56]{0:T(128)} %src_hbm.3, s32[1]{0:T(128)S(6)} %copy.18.count_hbm, bf16[1024,128]{1,0:T(8,128)(2,1)} %features_ref.1, bf16[128,128]{1,0:T(8,128)(2,1)} %w_self_ref.1, bf16[128,128]{1,0:T(8,128)(2,1)} %w_neigh_ref.1, ...), custom_call_target="tpu_custom_call" | custom-call | flops 939524096 | bytes 7340032 | tf_op jit(solution)/shard_map/own_tiles/pallas_call | solution.py:428
  14.3 2.1 %all-to-all-done.arrived_ref = f32[8,8,128]{2,1,0:T(8,128)S(1)} async-done(((f32[8,8,128]{2,1,0:T(8,128)}), f32[8,8,128]{2,1,0:T(8,128)S(1)}, u32[]{:S(2)}, u32[]{:S(2)}) %all-to-all-start) | async-done | bytes 32800 | tf_op jit(solution)/shard_map/all_to_all | solution.py:474
  16.5 0.0 copy-done
  16.5 0.0 copy-done.4
  16.5 0.0 copy-done.7
  16.5 0.0 copy-done.6
  16.5 0.0 copy-done.3
  16.5 0.0 copy-done.2
  16.5 0.0 copy-done.1
  16.5 0.0 copy-start.5
  16.5 0.0 copy-start.8
  16.6 0.0 copy-start.9
  16.6 3.7 %rest.1 = (bf16[1024,128]{1,0:T(8,128)(2,1)}, f32[1024,128]{1,0:T(8,128)S(1)}, bf16[288,128]{1,0:T(8,128)(2,1)S(1)}, f32[24,128]{1,0:T(8,128)S(1)}) custom-call(s32[56]{0:T(128)S(1)} %copy-done.6, s32[56]{0:T(128)S(1)} %copy-done.7, s32[1]{0:T(128)S(6)} %copy.18.count_hbm, s32[16]{0:T(128)S(1)} %bitcast.8, f32[8,8,128]{2,1,0:T(8,128)S(1)} %all-to-all-done.arrived_ref, ...), custom_call_target="tpu_custom_call" | custom-call | tf_op jit(solution)/shard_map/rest/pallas_call | solution.py:428
  20.3 1.8 %collective-permute-start = (bf16[288,128]{1,0:T(8,128)(2,1)S(1)}, bf16[288,128]{1,0:T(8,128)(2,1)S(1)}, u32[]{:S(2)}, u32[]{:S(2)}) collective-permute-start(bf16[288,128]{1,0:T(8,128)(2,1)S(1)} %get-tuple-element.28.sent_ref), channel_id=1, source_target_pairs={{0,8},{2,10},{4,12},{6,14},{8,0},{10,2},{12,4},{14,6},{1,9},{3,11}... | collective-permute-start | bytes 221192 | tf_op jit(solution)/shard_map/ppermute | solution.py:544
  22.1 3.5 %collective-permute-done.got_ref = bf16[288,128]{1,0:T(8,128)(2,1)S(1)} collective-permute-done((bf16[288,128]{1,0:T(8,128)(2,1)S(1)}, bf16[288,128]{1,0:T(8,128)(2,1)S(1)}, u32[]{:S(2)}, u32[]{:S(2)}) %collective-permute-start) | collective-permute-done | bytes 73760 | tf_op jit(solution)/shard_map/ppermute | solution.py:544
  25.6 0.0 collective-permute-start.1
  25.6 4.1 %collective-permute-start.2 = (bf16[288,128]{1,0:T(8,128)(2,1)S(1)}, bf16[288,128]{1,0:T(8,128)(2,1)S(1)}, u32[]{:S(2)}, u32[]{:S(2)}) collective-permute-start(bf16[288,128]{1,0:T(8,128)(2,1)S(1)} %get-tuple-element.33.sent_ref), channel_id=1, source_target_pairs={{0,4},{2,6},{4,0},{6,2},{8,12},{10,14},{12,8},{14,10},{1,5},{3,7},... | collective-permute-start | bytes 221192 | tf_op jit(solution)/shard_map/ppermute | solution.py:544
  29.8 2.9 %collective-permute-done.2.got_ref = bf16[288,128]{1,0:T(8,128)(2,1)S(1)} collective-permute-done((bf16[288,128]{1,0:T(8,128)(2,1)S(1)}, bf16[288,128]{1,0:T(8,128)(2,1)S(1)}, u32[]{:S(2)}, u32[]{:S(2)}) %collective-permute-start.2) | collective-permute-done | bytes 73760 | tf_op jit(solution)/shard_map/ppermute | solution.py:544
  32.8 0.1 collective-permute-start.3
  32.8 0.1 collective-permute-start.5
  32.9 2.0 %collective-permute-start.4 = (bf16[16,128]{1,0:T(8,128)(2,1)S(1)}, bf16[16,128]{1,0:T(8,128)(2,1)S(1)}, u32[]{:S(2)}, u32[]{:S(2)}) collective-permute-start(bf16[16,128]{1,0:T(8,128)(2,1)S(1)} %get-tuple-element.36), channel_id=1, source_target_pairs={{0,3},{1,2},{2,1},{3,0},{4,7},{5,6},{6,5},{7,4},{8,11},{9,10},{10,... | collective-permute-start | bytes 12296 | tf_op jit(solution)/shard_map/ppermute | solution.py:556
  35.0 0.0 collective-permute-done.1.other_partial_ref
  35.0 0.0 copy-done.5
  35.0 0.0 copy-done.8
  35.0 0.0 copy-done.9
  35.0 1.2 %prepare.1 = (f32[1024,128]{1,0:T(8,128)S(1)}, s32[20]{0:T(128)S(1)}) custom-call(s32[2,8]{1,0:T(2,128)S(1)} %bitcast.11, s32[8]{0:T(128)S(1)} %bitcast.13, s32[16]{0:T(128)S(1)} %bitcast.9, s32[16]{0:T(128)S(1)} %copy-done.9, f32[1024,128]{1,0:T(8,128)S(1)} %get-tuple-element.29.partial_ref, f32[1024,128]{1,0:T(8,128)S(1)} %collective-permute-done.1.other_partial_ref), custom_call_target="tpu_custom_call" | custom-call | flops 1000000 | bytes 4000000 | tf_op jit(solution)/shard_map/prepare/pallas_call | solution.py:428
  36.2 0.1 collective-permute-done.4.cross_ref
  36.3 0.0 collective-permute-done.5.other_keep_ref
  36.3 0.8 %collective-permute-done.3.got_ref = bf16[272,128]{1,0:T(8,128)(2,1)S(1)} collective-permute-done((bf16[272,128]{1,0:T(8,128)(2,1)S(1)}, bf16[272,128]{1,0:T(8,128)(2,1)S(1)}, u32[]{:S(2)}, u32[]{:S(2)}) %collective-permute-start.3) | collective-permute-done | bytes 69664 | tf_op jit(solution)/shard_map/ppermute | solution.py:555
  37.1 1.4 %final.1 = (f32[128,128]{1,0:T(8,128)}, f32[128,128]{1,0:T(8,128)}, f32[1,128]{1,0:T(1,128)}, bf16[1024,128]{1,0:T(8,128)(2,1)}) custom-call(s32[20]{0:T(128)S(1)} %get-tuple-element.30.target_hbm, bf16[272,128]{1,0:T(8,128)(2,1)S(1)} %get-tuple-element.35.sent_ref, bf16[272,128]{1,0:T(8,128)(2,1)S(1)} %collective-permute-done.3.got_ref, ...), custom_call_target="tpu_custom_call" | custom-call | tf_op jit(solution)/shard_map/final/pallas_call | solution.py:428
  (2 shorter events, 0.1 us)
Async XLA Ops:
  0.6 15.9 %copy-start = (bf16[1024,128]{1,0:T(8,128)(2,1)S(1)}, bf16[1024,128]{1,0:T(8,128)(2,1)}, u32[]{:S(2)}) copy-start(bf16[1024,128]{1,0:T(8,128)(2,1)} %features_ref.1) | copy-start | bytes 786436
  0.6 15.8 %copy-start.4 = (s32[16,1]{0,1:T(1,128)S(1)}, s32[16,1]{0,1:T(1,128)}, u32[]{:S(2)}) copy-start(s32[16,1]{0,1:T(1,128)} %param.24) | copy-start | bytes 196
  0.7 15.8 %copy-start.7 = (s32[56]{0:T(128)S(1)}, s32[56]{0:T(128)}, u32[]{:S(2)}) copy-start(s32[56]{0:T(128)} %src_hbm.3) | copy-start | bytes 676
  0.7 15.8 %copy-start.6 = (s32[56]{0:T(128)S(1)}, s32[56]{0:T(128)}, u32[]{:S(2)}) copy-start(s32[56]{0:T(128)} %dst_hbm.3) | copy-start | bytes 676
  0.7 15.8 %copy-start.3 = (bf16[128,128]{1,0:T(8,128)(2,1)S(1)}, bf16[128,128]{1,0:T(8,128)(2,1)}, u32[]{:S(2)}) copy-start(bf16[128,128]{1,0:T(8,128)(2,1)} %w_neigh_ref.1) | copy-start | bytes 98308
  0.7 15.8 %copy-start.2 = (bf16[128,128]{1,0:T(8,128)(2,1)S(1)}, bf16[128,128]{1,0:T(8,128)(2,1)}, u32[]{:S(2)}) copy-start(bf16[128,128]{1,0:T(8,128)(2,1)} %w_self_ref.1) | copy-start | bytes 98308
  0.7 15.8 %copy-start.1 = (bf16[1024,128]{1,0:T(8,128)(2,1)S(1)}, bf16[1024,128]{1,0:T(8,128)(2,1)}, u32[]{:S(2)}) copy-start(bf16[1024,128]{1,0:T(8,128)(2,1)} %cotangent_ref.1) | copy-start | bytes 786436
  2.5 14.0 %all-to-all-start = ((f32[8,8,128]{2,1,0:T(8,128)}), f32[8,8,128]{2,1,0:T(8,128)S(1)}, u32[]{:S(2)}, u32[]{:S(2)}) async-start(f32[8,8,128]{2,1,0:T(8,128)} %gather.1), calls=%async_computation | async-start | bytes 65536 | tf_op jit(solution)/shard_map/all_to_all | solution.py:474
  16.5 18.4 %copy-start.5 = (s32[1,8,2]{1,2,0:T(2,128)S(1)}, s32[1,8,2]{1,2,0:T(2,128)}, u32[]{:S(2)}) copy-start(s32[1,8,2]{1,2,0:T(2,128)} %param.22) | copy-start | bytes 196
  16.5 18.4 %copy-start.8 = (s32[1,8]{1,0:T(1,128)S(1)}, s32[1,8]{1,0:T(1,128)}, u32[]{:S(2)}) copy-start(s32[1,8]{1,0:T(1,128)} %param.23) | copy-start | bytes 100
  16.6 18.4 %copy-start.9 = (s32[16]{0:T(128)S(1)}, s32[16]{0:T(128)}, u32[]{:S(2)}) copy-start(s32[16]{0:T(128)} %hub_row_ref.1) | copy-start | bytes 196
  20.3 5.3 %collective-permute-start = (bf16[288,128]{1,0:T(8,128)(2,1)S(1)}, bf16[288,128]{1,0:T(8,128)(2,1)S(1)}, u32[]{:S(2)}, u32[]{:S(2)}) collective-permute-start(bf16[288,128]{1,0:T(8,128)(2,1)S(1)} %get-tuple-element.28.sent_ref), channel_id=1, source_target_pairs={{0,8},{2,10},{4,12},{6,14},{8,0},{10,2},{12,4},{14,6},{1,9},{3,11}... | collective-permute-start | bytes 221192 | tf_op jit(solution)/shard_map/ppermute | solution.py:544
  25.6 9.4 %collective-permute-start.1 = (f32[1024,128]{1,0:T(8,128)S(1)}, f32[1024,128]{1,0:T(8,128)S(1)}, u32[]{:S(2)}, u32[]{:S(2)}) collective-permute-start(f32[1024,128]{1,0:T(8,128)S(1)} %get-tuple-element.29.partial_ref), channel_id=1, source_target_pairs={{0,1},{1,0},{2,3},{3,2},{4,5},{5,4},{6,7},{7,6},{8,9},{9,8},{10,11... | collective-permute-start | bytes 1572872 | tf_op jit(solution)/shard_map/ppermute | solution.py:558
  25.6 7.1 %collective-permute-start.2 = (bf16[288,128]{1,0:T(8,128)(2,1)S(1)}, bf16[288,128]{1,0:T(8,128)(2,1)S(1)}, u32[]{:S(2)}, u32[]{:S(2)}) collective-permute-start(bf16[288,128]{1,0:T(8,128)(2,1)S(1)} %get-tuple-element.33.sent_ref), channel_id=1, source_target_pairs={{0,4},{2,6},{4,0},{6,2},{8,12},{10,14},{12,8},{14,10},{1,5},{3,7},... | collective-permute-start | bytes 221192 | tf_op jit(solution)/shard_map/ppermute | solution.py:544
  32.8 4.4 %collective-permute-start.3 = (bf16[272,128]{1,0:T(8,128)(2,1)S(1)}, bf16[272,128]{1,0:T(8,128)(2,1)S(1)}, u32[]{:S(2)}, u32[]{:S(2)}) collective-permute-start(bf16[272,128]{1,0:T(8,128)(2,1)S(1)} %get-tuple-element.35.sent_ref), channel_id=1, source_target_pairs={{0,2},{2,0},{4,6},{6,4},{8,10},{10,8},{12,14},{14,12},{1,3},{3,1},... | collective-permute-start | bytes 208904 | tf_op jit(solution)/shard_map/ppermute | solution.py:555
  32.8 3.5 %collective-permute-start.5 = (f32[12,128]{1,0:T(8,128)S(1)}, f32[12,128]{1,0:T(8,128)S(1)}, u32[]{:S(2)}, u32[]{:S(2)}) collective-permute-start(f32[12,128]{1,0:T(8,128)S(1)} %get-tuple-element.37.keep_ref), channel_id=1, source_target_pairs={{0,1},{1,0},{2,3},{3,2},{4,5},{5,4},{6,7},{7,6},{8,9},{9,8},{10,11... | collective-permute-start | bytes 18440 | tf_op jit(solution)/shard_map/ppermute | solution.py:557
  32.9 3.4 %collective-permute-start.4 = (bf16[16,128]{1,0:T(8,128)(2,1)S(1)}, bf16[16,128]{1,0:T(8,128)(2,1)S(1)}, u32[]{:S(2)}, u32[]{:S(2)}) collective-permute-start(bf16[16,128]{1,0:T(8,128)(2,1)S(1)} %get-tuple-element.36), channel_id=1, source_target_pairs={{0,3},{1,2},{2,1},{3,0},{4,7},{5,6},{6,5},{7,4},{8,11},{9,10},{10,... | collective-permute-start | bytes 12296 | tf_op jit(solution)/shard_map/ppermute | solution.py:556
